TPU v7x, 128 devices: a whole 4x4x4 slice. The times are simulated.
128 devices in a mesh: clip: 32 (over x, z, y_lo), head: 4 (over y_hi, core).
Axes of the slice: x: 4, y: 4 (y_hi: 2, y_lo: 2; y = y_hi * 2 + y_lo), z: 4, core: 2. Of those that a mesh axis runs over, the one named last changes fastest.
Arguments:
- tokens: bfloat16 [50176, 768], P(('clip', 'head')), may hold values from -6 to 6
- cube_mask: int32 [32, 196], P('clip'), may hold values 0 or 1
- mask_token: bfloat16 [768], P(('clip', 'head')), may hold values from -4 to 4
- norm1_gain: bfloat16 [768], P(('clip', 'head')), may hold values from 0.099609375 to 1.8984375
- norm1_bias: bfloat16 [768], P(('clip', 'head')), may hold values from -3 to 3
- w_qkv: bfloat16 [768, 2304], P(None, 'head'), may hold values from -0.21875 to 0.21875
- qv_bias: bfloat16 [2, 768], P(None, 'head'), may hold values from -3 to 3
- w_out: bfloat16 [768, 768], P('head'), may hold values from -3.5 to 3.5
- proj_bias: bfloat16 [768], P(('clip', 'head')), may hold values from -3 to 3
- norm2_gain: bfloat16 [768], P(('clip', 'head')), may hold values from 0.099609375 to 1.8984375
- norm2_bias: bfloat16 [768], P(('clip', 'head')), may hold values from -3 to 3
- w_fc1: bfloat16 [768, 3072], P(None, ('clip', 'head')), may hold values from -0.21875 to 0.21875
- fc1_bias: bfloat16 [3072], P(('clip', 'head')), may hold values from -3 to 3
- w_fc2: bfloat16 [3072, 768], P(('clip', 'head')), may hold values from -0.109375 to 0.109375
- fc2_bias: bfloat16 [768], P(('clip', 'head')), may hold values from -3 to 3
- cotangent: bfloat16 [50176, 768], P(('clip', 'head')), may hold values from -6 to 6
Outputs:
- block_out: float32 [50176, 768], P(('clip', 'head'))
- tokens_grad: float32 [50176, 768], P(('clip', 'head'))
- mask_token_grad: float32 [768], P(('clip', 'head'))
- norm1_gain_grad: float32 [768], P(('clip', 'head'))
- norm1_bias_grad: float32 [768], P(('clip', 'head'))
- w_qkv_grad: float32 [768, 2304], P(None, 'head')
- qv_bias_grad: float32 [2, 768], P(None, 'head')
- w_out_grad: float32 [768, 768], P('head')
- proj_bias_grad: float32 [768], P(('clip', 'head'))
- norm2_gain_grad: float32 [768], P(('clip', 'head'))
- norm2_bias_grad: float32 [768], P(('clip', 'head'))
- w_fc1_grad: float32 [768, 3072], P(None, ('clip', 'head'))
- fc1_bias_grad: float32 [3072], P(('clip', 'head'))
- w_fc2_grad: float32 [3072, 768], P(('clip', 'head'))
- fc2_bias_grad: float32 [768], P(('clip', 'head'))
Inputs may be any that keep to these rules, and one draw needn't show every extreme that they name: `cube_mask`: 1 marks a masked cube of 2 x 2 x 2 tubes.
All inputs are finite; a program needn't handle non-finite values. No bound on the sum of `cube_mask` on one device may be relied on, other than what follows from the above.
Results may differ from a plain program's by a relative error of at most 0.025.
Values may be sent and summed in bfloat16 or wider, within the bound.
A program may use at most 256 MiB of HBM per device.

v0:
```python
from functools import partial
import math

import jax
import jax.numpy as jnp
from jax import lax
from jax.sharding import PartitionSpec as P

HEAD_DIM = 64
GRID = 14
TOK = 1568


epsilon = 1e-06


def normalize(values, gain_vec, shift_vec):
    average = jnp.mean(values, axis=-1, keepdims=True)
    centered = values - average
    inverse = lax.rsqrt(jnp.mean(centered * centered, axis=-1, keepdims=True) + epsilon)
    unit = centered * inverse
    return (unit * gain_vec + shift_vec, unit, inverse)


def normalize_back(grad_normed, unit, inverse, gain_vec):
    scaled = grad_normed * gain_vec
    return inverse * (
        scaled
        - jnp.mean(scaled, axis=-1, keepdims=True)
        - unit * jnp.mean(scaled * unit, axis=-1, keepdims=True)
    )


def contract_rows(left, right):
    return lax.dot_general(
        left, right, (((0,), (0,)), ((), ())), preferred_element_type=jnp.float32
    )


def contract_last(left, right):
    return lax.dot_general(
        left, right, (((1,), (1,)), ((), ())), preferred_element_type=jnp.float32
    )


def attend_block(block):
    query = block[:, :, 0]
    keys = block[:, :, 1]
    values = block[:, :, 2]
    scores = jnp.einsum("qhe,khe->hqk", query, keys, preferred_element_type=jnp.float32) * (
        1.0 / math.sqrt(HEAD_DIM)
    )
    log_total = jax.nn.logsumexp(scores, axis=-1)
    weights = jnp.exp(scores - log_total[:, :, None]).astype(jnp.bfloat16)
    mixed = jnp.einsum("hqk,khe->qhe", weights, values, preferred_element_type=jnp.float32)
    return (mixed.astype(jnp.bfloat16), log_total)


def attend_back(inputs):
    block, log_total, grad_mixed = inputs
    score_scale = 1.0 / math.sqrt(HEAD_DIM)
    query = block[:, :, 0]
    keys = block[:, :, 1]
    values = block[:, :, 2]
    scores = (
        jnp.einsum("qhe,khe->hqk", query, keys, preferred_element_type=jnp.float32) * score_scale
    )
    soft_weights = jnp.exp(scores - log_total[:, :, None])
    soft_low = soft_weights.astype(jnp.bfloat16)
    grad_values = jnp.einsum(
        "hqk,qhe->khe", soft_low, grad_mixed, preferred_element_type=jnp.float32
    )
    grad_soft = jnp.einsum("qhe,khe->hqk", grad_mixed, values, preferred_element_type=jnp.float32)
    grad_scores = soft_weights * (
        grad_soft - jnp.sum(soft_weights * grad_soft, axis=-1, keepdims=True)
    )
    grad_scores = grad_scores.astype(jnp.bfloat16)
    grad_query = (
        jnp.einsum("hqk,khe->qhe", grad_scores, keys, preferred_element_type=jnp.float32)
        * score_scale
    )
    grad_keys = (
        jnp.einsum("hqk,qhe->khe", grad_scores, query, preferred_element_type=jnp.float32)
        * score_scale
    )
    return jnp.stack([grad_query, grad_keys, grad_values], axis=2).astype(jnp.bfloat16)


def body(
    tokens,
    cube_mask,
    mask_token,
    norm1_gain,
    norm1_bias,
    w_qkv,
    qv_bias,
    w_out,
    proj_bias,
    norm2_gain,
    norm2_bias,
    w_fc1,
    fc1_bias,
    w_fc2,
    fc2_bias,
    cotangent,
):
    head_count = lax.axis_size("head")
    head_index = lax.axis_index("head")
    row_count = tokens.shape[0]
    group_rows = row_count * head_count
    local_heads = w_qkv.shape[1] // (3 * HEAD_DIM)
    clips_here = cube_mask.shape[0]
    (
        full_fc1,
        full_fc1_bias,
        full_fc2,
        full_mask,
        full_gain1,
        full_shift1,
        full_proj_bias,
        full_gain2,
        full_shift2,
        full_fc2_bias,
    ) = (
        lax.all_gather(w_fc1, ("clip", "head"), axis=1, tiled=True),
        lax.all_gather(fc1_bias, ("clip", "head"), axis=0, tiled=True),
        lax.all_gather(w_fc2, ("clip", "head"), axis=0, tiled=True),
        lax.all_gather(mask_token, ("clip", "head"), axis=0, tiled=True),
        lax.all_gather(norm1_gain, ("clip", "head"), axis=0, tiled=True),
        lax.all_gather(norm1_bias, ("clip", "head"), axis=0, tiled=True),
        lax.all_gather(proj_bias, ("clip", "head"), axis=0, tiled=True),
        lax.all_gather(norm2_gain, ("clip", "head"), axis=0, tiled=True),
        lax.all_gather(norm2_bias, ("clip", "head"), axis=0, tiled=True),
        lax.all_gather(fc2_bias, ("clip", "head"), axis=0, tiled=True),
    )
    gain1 = full_gain1.astype(jnp.float32)
    shift1 = full_shift1.astype(jnp.float32)
    gain2 = full_gain2.astype(jnp.float32)
    shift2 = full_shift2.astype(jnp.float32)
    index_rows = head_index * row_count + jnp.arange(row_count, dtype=jnp.int32)
    clip_of = index_rows // TOK
    within = index_rows % TOK
    plane_size = GRID * GRID
    half_grid = GRID // 2
    frame_index = within // plane_size
    spot_index = within % plane_size
    cube_index = (
        frame_index // 2 * half_grid * half_grid
        + spot_index // GRID // 2 * half_grid
        + spot_index % GRID // 2
    )
    masked = jnp.take(cube_mask.reshape(-1), clip_of * cube_mask.shape[1] + cube_index) > 0
    start = jnp.where(
        masked[:, None], full_mask.astype(jnp.float32)[None, :], tokens.astype(jnp.float32)
    )
    normed1, unit1, inverse1 = normalize(start, gain1, shift1)
    normed1_low = normed1.astype(jnp.bfloat16)
    rows_all = lax.all_gather(normed1_low, "head", axis=0, tiled=True)
    packed = jnp.dot(rows_all, w_qkv, preferred_element_type=jnp.float32).reshape(
        group_rows, local_heads, 3, HEAD_DIM
    )
    bias_pair = qv_bias.astype(jnp.float32).reshape(2, local_heads, HEAD_DIM)
    bias_full = jnp.stack([bias_pair[0], jnp.zeros_like(bias_pair[0]), bias_pair[1]], axis=1)
    packed_low = (packed + bias_full[None]).astype(jnp.bfloat16)
    blocks = packed_low.reshape(clips_here, TOK, local_heads, 3, HEAD_DIM)
    mixed_blocks, log_totals = lax.map(attend_block, blocks)
    mixed_low = mixed_blocks.reshape(group_rows, local_heads * HEAD_DIM)
    total_branch = lax.psum(
        jnp.dot(mixed_low, w_out, preferred_element_type=jnp.float32).astype(jnp.bfloat16), "head"
    ).astype(jnp.float32)
    branch = lax.dynamic_slice_in_dim(total_branch, head_index * row_count, row_count, 0)
    middle = start + branch + full_proj_bias.astype(jnp.float32)[None, :]
    normed2, unit2, inverse2 = normalize(middle, gain2, shift2)
    normed2_low = normed2.astype(jnp.bfloat16)
    inner = (
        jnp.dot(normed2_low, full_fc1, preferred_element_type=jnp.float32)
        + full_fc1_bias.astype(jnp.float32)[None, :]
    )
    active, gelu_back = jax.vjp(partial(jax.nn.gelu, approximate=False), inner)
    active_low = active.astype(jnp.bfloat16)
    outer = jnp.dot(active_low, full_fc2, preferred_element_type=jnp.float32)
    block_out = middle + outer + full_fc2_bias.astype(jnp.float32)[None, :]
    back_fc1, back_fc2 = (
        lax.all_gather(w_fc1, ("clip", "head"), axis=1, tiled=True),
        lax.all_gather(w_fc2, ("clip", "head"), axis=0, tiled=True),
    )
    grad_out = cotangent.astype(jnp.float32)
    grad_fc2 = contract_rows(active_low, cotangent)
    grad_fc2_bias = jnp.sum(grad_out, axis=0)
    grad_active = contract_last(cotangent, back_fc2)
    grad_inner = gelu_back(grad_active)[0].astype(jnp.bfloat16)
    grad_fc1 = contract_rows(normed2_low, grad_inner)
    grad_fc1_bias = jnp.sum(grad_inner.astype(jnp.float32), axis=0)
    grad_normed2 = contract_last(grad_inner, back_fc1)
    grad_gain2 = jnp.sum(grad_normed2 * unit2, axis=0)
    grad_shift2 = jnp.sum(grad_normed2, axis=0)
    grad_middle = grad_out + normalize_back(grad_normed2, unit2, inverse2, gain2)
    grad_proj_bias = jnp.sum(grad_middle, axis=0)
    grad_branch = grad_middle.astype(jnp.bfloat16)
    grad_rows = lax.all_gather(grad_branch, "head", axis=0, tiled=True)
    grad_w_out = contract_rows(mixed_low, grad_rows)
    grad_mixed = contract_last(grad_rows, w_out).astype(jnp.bfloat16)
    grad_blocks = lax.map(
        attend_back,
        (blocks, log_totals, grad_mixed.reshape(clips_here, TOK, local_heads, HEAD_DIM)),
    )
    grad_packed = grad_blocks.reshape(group_rows, local_heads * 3 * HEAD_DIM)
    grad_w_qkv = contract_rows(rows_all, grad_packed)
    grad_bias_all = jnp.sum(grad_packed.astype(jnp.float32), axis=0).reshape(
        local_heads, 3, HEAD_DIM
    )
    grad_qv_bias = jnp.stack(
        [grad_bias_all[:, 0].reshape(-1), grad_bias_all[:, 2].reshape(-1)], axis=0
    )
    total_input = lax.psum(contract_last(grad_packed, w_qkv).astype(jnp.bfloat16), "head").astype(
        jnp.float32
    )
    grad_normed1 = lax.dynamic_slice_in_dim(total_input, head_index * row_count, row_count, 0)
    grad_gain1 = jnp.sum(grad_normed1 * unit1, axis=0)
    grad_shift1 = jnp.sum(grad_normed1, axis=0)
    grad_start = grad_middle + normalize_back(grad_normed1, unit1, inverse1, gain1)
    tokens_grad = jnp.where(masked[:, None], 0.0, grad_start)
    grad_mask = jnp.sum(jnp.where(masked[:, None], grad_start, 0.0), axis=0)
    w_qkv_grad, w_out_grad, qv_bias_grad = (
        lax.psum(grad_w_qkv.astype(jnp.bfloat16), "clip").astype(jnp.float32),
        lax.psum(grad_w_out.astype(jnp.bfloat16), "clip").astype(jnp.float32),
        lax.psum(grad_qv_bias.astype(jnp.bfloat16), "clip").astype(jnp.float32),
    )
    (
        w_fc1_grad,
        fc1_bias_grad,
        w_fc2_grad,
        mask_token_grad,
        norm1_gain_grad,
        norm1_bias_grad,
        proj_bias_grad,
        norm2_gain_grad,
        norm2_bias_grad,
        fc2_bias_grad,
    ) = (
        lax.psum_scatter(grad_fc1, ("clip", "head"), scatter_dimension=1, tiled=True),
        lax.psum_scatter(grad_fc1_bias, ("clip", "head"), scatter_dimension=0, tiled=True),
        lax.psum_scatter(grad_fc2, ("clip", "head"), scatter_dimension=0, tiled=True),
        lax.psum_scatter(grad_mask, ("clip", "head"), scatter_dimension=0, tiled=True),
        lax.psum_scatter(grad_gain1, ("clip", "head"), scatter_dimension=0, tiled=True),
        lax.psum_scatter(grad_shift1, ("clip", "head"), scatter_dimension=0, tiled=True),
        lax.psum_scatter(grad_proj_bias, ("clip", "head"), scatter_dimension=0, tiled=True),
        lax.psum_scatter(grad_gain2, ("clip", "head"), scatter_dimension=0, tiled=True),
        lax.psum_scatter(grad_shift2, ("clip", "head"), scatter_dimension=0, tiled=True),
        lax.psum_scatter(grad_fc2_bias, ("clip", "head"), scatter_dimension=0, tiled=True),
    )
    return (
        block_out,
        tokens_grad,
        mask_token_grad,
        norm1_gain_grad,
        norm1_bias_grad,
        w_qkv_grad,
        qv_bias_grad,
        w_out_grad,
        proj_bias_grad,
        norm2_gain_grad,
        norm2_bias_grad,
        w_fc1_grad,
        fc1_bias_grad,
        w_fc2_grad,
        fc2_bias_grad,
    )


def solution(mesh):
    in_specs = (
        P(("clip", "head"), None),
        P("clip", None),
        P(("clip", "head")),
        P(("clip", "head")),
        P(("clip", "head")),
        P(None, "head"),
        P(None, "head"),
        P("head", None),
        P(("clip", "head")),
        P(("clip", "head")),
        P(("clip", "head")),
        P(None, ("clip", "head")),
        P(("clip", "head")),
        P(("clip", "head"), None),
        P(("clip", "head")),
        P(("clip", "head"), None),
    )
    out_specs = (
        P(("clip", "head"), None),
        P(("clip", "head"), None),
        P(("clip", "head")),
        P(("clip", "head")),
        P(("clip", "head")),
        P(None, "head"),
        P(None, "head"),
        P("head", None),
        P(("clip", "head")),
        P(("clip", "head")),
        P(("clip", "head")),
        P(None, ("clip", "head")),
        P(("clip", "head")),
        P(("clip", "head"), None),
        P(("clip", "head")),
    )
    return jax.shard_map(body, mesh=mesh, in_specs=in_specs, out_specs=out_specs, check_vma=False)
```

profile of v0, /device:TPU:0, one launch (start us, length us, event | category | flops | bytes accessed | tf_op | source)
XLA Modules:
  0.0 2066.4 jit_solution(18007368682445462969)
XLA Ops:
  8.2 3.7 gather_fusion
  18.7 68.6 %all-reduce.17 = (bf16[768]{0:T(1024)(128)(2,1)S(1)}, bf16[768]{0:T(1024)(128)(2,1)S(1)}, bf16[768]{0:T(1024)(128)(2,1)S(1)}, bf16[768]{0:T(1024)(128)(2,1)S(1)}...) all-reduce(bf16[768]{0:T(1024)(128)(2,1)S(1)} %dynamic-update-slice, ...), channel_id=1, replica_groups=mesh['clip'=32,'head'=4] {'clip','head'}, use_global_device_ids=true, to_apply=%add.5 | all-reduce | flops 8448 | bytes 33792
  90.6 24.1 %all-gather.5.cloned.1.call-done = bf16[1568,768]{1,0:T(8,128)(2,1)} async-done(((bf16[392,768]{1,0:T(8,128)(2,1)}), bf16[1568,768]{1,0:T(8,128)(2,1)}) %all-gather.5.cloned.1.call-update) | async-done | bytes 2408464 | tf_op jit(solution)/shard_map/all_gather | solution.py:158
  114.7 3.5 fusion.54
  118.5 11.8 multiply_reduce_fusion.1
  130.2 12.7 exponential_reduce_fusion
  143.0 15.2 convolution_convert_fusion.2
  163.2 63.4 %all-reduce.23.cloned.1.call-done = bf16[1568,768]{1,0:T(8,128)(2,1)} async-done(((bf16[1568,768]{1,0:T(8,128)(2,1)}), bf16[1568,768]{1,0:T(8,128)(2,1)}) %all-reduce.23.cloned.1.call-update) | async-done | bytes 2408464 | tf_op jit(solution)/shard_map/psum | solution.py:168
  229.7 166.7 %all-gather.7.cloned.1.call-done = bf16[768,3072]{0,1:T(8,128)(2,1)} async-done(((bf16[768,24]{0,1:T(8,128)(2,1)}), bf16[768,3072]{0,1:T(8,128)(2,1)}) %all-gather.7.cloned.1.call-update) | async-done | bytes 4718608 | tf_op jit(solution)/shard_map/all_gather | solution.py:125
  396.4 7.2 fusion.47
  403.6 193.7 %all-gather.9.cloned.1.call-done = bf16[3072,768]{1,0:T(8,128)(2,1)} async-done(((bf16[24,768]{1,0:T(8,128)(2,1)}), bf16[3072,768]{1,0:T(8,128)(2,1)}) %all-gather.9.cloned.1.call-update) | async-done | bytes 4718608 | tf_op jit(solution)/shard_map/all_gather | solution.py:127
  597.3 15.8 convert_reduce_fusion
  618.5 26.8 %all-gather.11.cloned.1.call-done = bf16[1568,768]{1,0:T(8,128)(2,1)} async-done(((bf16[392,768]{1,0:T(8,128)(2,1)}), bf16[1568,768]{1,0:T(8,128)(2,1)}) %all-gather.11.cloned.1.call-update) | async-done | bytes 2408464 | tf_op jit(solution)/shard_map/all_gather | solution.py:200
  645.3 3.5 convolution_convert_fusion.3
  648.8 14.0 convolution_bitcast_fusion
  662.8 23.8 %multiply_reduce_fusion = (f32[3,1568]{1,0:T(4,128)S(1)}, f32[3,1568,1568]{1,2,0:T(8,128)}) fusion(f32[3,1568,1568]{1,2,0:T(8,128)} %get-tuple-element.83, f32[3,1568]{1,0:T(4,128)S(1)} %log_add_fusion, bf16[1568,3,64]{0,2,1:T(8,128)(2,1)} %bitcast.74, bf16[1568,3,3,64]{0,3,1,2:T(8,128)(2,1)S(1)} %fusion.7), kind=kOutput, calls=%fused_computation.2 | convolution fusion | flops 973610368 | bytes 60293504 | tf_op jit(solution)/shard_map/while/body/eval_jaxpr/qhe,khe->hqk/dot_general | solution.py:73
  686.6 25.6 %multiply_convert_fusion = bf16[3,1568,1568]{1,2,0:T(8,128)(2,1)} fusion(f32[3,1568,1568]{1,2,0:T(8,128)} %get-tuple-element.86, f32[3,1568,1568]{1,2,0:T(8,128)} %get-tuple-element.83, f32[3,1568]{1,0:T(4,128)S(1)} %get-tuple-element.85, f32[3,1568]{1,0:T(4,128)S(1)} %log_add_fusion), kind=kLoop, calls=%fused_computation.1 | loop fusion | flops 36879360 | bytes 73796352 | tf_op jit(solution)/shard_map/while/body/eval_jaxpr/convert_element_type | solution.py:77
  712.2 10.2 fusion.9
  722.3 8.0 fusion.8
  734.3 2.7 convolution_convert_fusion.4
  737.1 3.7 convolution_convert_fusion
  741.1 8.5 fusion.46
  749.7 5.0 multiply_convert_fusion.1
  756.2 5.1 fusion.55
  762.0 6.3 fusion.15
  768.4 82.2 %psum.38 = bf16[2,192]{1,0:T(2,128)(2,1)S(1)} all-reduce(bf16[2,192]{1,0:T(2,128)(2,1)S(1)} %pad_maximum_fusion.1), channel_id=1, replica_groups=mesh['clip'=32,'head'=4] {'clip'}, use_global_device_ids=true, to_apply=%region_21.22 | all-reduce | flops 384 | bytes 1536 | tf_op jit(solution)/shard_map/psum | solution.py:227
  851.3 190.6 %all-reduce.27.cloned.1.call-done = (bf16[768,576]{0,1:T(8,128)(2,1)}, bf16[192,768]{1,0:T(8,128)(2,1)}) async-done(((bf16[768,576]{0,1:T(8,128)(2,1)}, bf16[192,768]{1,0:T(8,128)(2,1)}), (bf16[768,576]{0,1:T(8,128)(2,1)}, bf16[192,768]{1,0:T(8,128)(2,1)})) %all-reduce.27.cloned.1.call-update) | async-done | bytes 1179664 | tf_op jit(solution)/shard_map/psum | solution.py:225
  1046.2 62.0 %all-reduce.25.cloned.1.call-done = bf16[1568,768]{1,0:T(8,128)(2,1)} async-done(((bf16[1568,768]{1,0:T(8,128)(2,1)}), bf16[1568,768]{1,0:T(8,128)(2,1)}) %all-reduce.25.cloned.1.call-update) | async-done | bytes 2408464 | tf_op jit(solution)/shard_map/psum | solution.py:215
  1110.1 2.7 select_reduce_fusion
  1112.8 69.5 %all-reduce.16 = (f32[768]{0:T(1024)S(1)}, f32[768]{0:T(1024)S(1)}, f32[768]{0:T(1024)S(1)}, f32[768]{0:T(1024)S(1)}, f32[768]{0:T(1024)S(1)}, /*index=5*/f32[76...) all-reduce(f32[768]{0:T(1024)S(1)} %get-tuple-element.77, ...), channel_id=2, replica_groups=mesh['clip'=32,'head'=4] {'clip','head'}, use_global_device_ids=true, to_apply=%region_14.15.clone | all-reduce | flops 8448 | bytes 67584
  1189.4 217.6 %reduce-scatter.3.cloned.1.call-done = f32[768,24]{0,1:T(8,128)} async-done(((f32[768,3072]{0,1:T(8,128)}), f32[768,24]{0,1:T(8,128)}) %reduce-scatter.3.cloned.1.call-update) | async-done | bytes 73744 | tf_op jit(solution)/shard_map/reduce_scatter | solution.py:241
  1406.9 651.9 %reduce-scatter.5.cloned.1.call-done = f32[24,768]{1,0:T(8,128)} async-done(((f32[3072,768]{1,0:T(8,128)}), f32[24,768]{1,0:T(8,128)}) %reduce-scatter.5.cloned.1.call-update) | async-done | bytes 73744 | tf_op jit(solution)/shard_map/reduce_scatter | solution.py:243
  (138 shorter events, 44.3 us)
Async XLA Ops:
  8.0 106.7 %copy-start = (bf16[768,576]{0,1:T(8,128)(2,1)S(1)}, bf16[768,576]{0,1:T(8,128)(2,1)}, u32[]{:S(2)}) copy-start(bf16[768,576]{0,1:T(8,128)(2,1)} %param.21) | copy-start | bytes 2654212
  8.0 79.3 %copy-start.1 = (bf16[392,768]{1,0:T(8,128)(2,1)S(1)}, bf16[392,768]{1,0:T(8,128)(2,1)}, u32[]{:S(2)}) copy-start(bf16[392,768]{1,0:T(8,128)(2,1)} %param.16) | copy-start | bytes 1806340
  8.0 106.7 %all-gather.5.cloned.1.call-start = ((), (), s32[]{:S(2)}) async-start(), calls=%async_computation.2 | async-start | bytes 3010560 | tf_op jit(solution)/shard_map/all_gather | solution.py:158
  8.2 82.1 %copy-start.19 = (bf16[2,192]{1,0:T(2,128)(2,1)S(1)}, bf16[2,192]{1,0:T(2,128)(2,1)}, u32[]{:S(2)}) copy-start(bf16[2,192]{1,0:T(2,128)(2,1)} %param.22) | copy-start | bytes 2308
  88.1 30.1 %copy-start.16 = (f32[392]{0:T(512)}, f32[392]{0:T(512)S(1)}, u32[]{:S(2)}) copy-start(f32[392]{0:T(512)S(1)} %add_rsqrt_fusion.1) | copy-start | bytes 4708
  88.1 0.6 copy-start.12
  89.9 136.6 %all-reduce.23.cloned.1.call-start = ((), (), s32[]{:S(2)}) async-start(), calls=%async_computation.3 | async-start | bytes 4816896 | tf_op jit(solution)/shard_map/psum | solution.py:168
  143.0 16.1 copy-start.11
  158.2 0.8 copy-start.4
  161.4 235.0 %all-gather.7.cloned.1.call-start = ((), (), s32[]{:S(2)}) async-start(), calls=%async_computation.4 | async-start | bytes 4755456 | tf_op jit(solution)/shard_map/all_gather | solution.py:125
  162.0 435.3 %all-gather.9.cloned.1.call-start = ((), (), s32[]{:S(2)}) async-start(), calls=%async_computation.5 | async-start | bytes 4755456 | tf_op jit(solution)/shard_map/all_gather | solution.py:127
  162.6 482.7 %all-gather.11.cloned.1.call-start = ((), (), s32[]{:S(2)}) async-start(), calls=%async_computation.6 | async-start | bytes 3010560 | tf_op jit(solution)/shard_map/all_gather | solution.py:200
  597.3 15.8 copy-start.8
  597.3 15.8 copy-start.20
  613.1 2.4 copy-start.23
  613.1 2.4 copy-start.9
  616.4 1.0 copy-start.2
  618.3 423.6 %all-reduce.27.cloned.1.call-start = ((), (), s32[]{:S(2)}) async-start(), calls=%async_computation.10 | async-start | bytes 2359296 | tf_op jit(solution)/shard_map/psum | solution.py:225
  722.3 8.0 copy-start.6
  730.8 1.1 copy-start.5
  730.8 1.9 copy-start.22
  732.7 1.7 copy-start.21
  737.1 371.2 %all-reduce.25.cloned.1.call-start = ((), (), s32[]{:S(2)}) async-start(), calls=%async_computation.7 | async-start | bytes 4816896 | tf_op jit(solution)/shard_map/psum | solution.py:215
  740.8 666.1 %reduce-scatter.3.cloned.1.call-start = ((), (), s32[]{:S(2)}) async-start(), calls=%async_computation.8 | async-start | bytes 9510912 | tf_op jit(solution)/shard_map/reduce_scatter | solution.py:241
  749.6 1309.2 %reduce-scatter.5.cloned.1.call-start = ((), (), s32[]{:S(2)}) async-start(), calls=%async_computation.9 | async-start | bytes 9510912 | tf_op jit(solution)/shard_map/reduce_scatter | solution.py:243
  749.7 6.5 copy-start.10
  754.7 1.5 copy-start.7
  761.3 0.7 copy-start.18
  768.2 340.0 %copy-start.13 = (f32[768]{0:T(1024)S(1)}, f32[768]{0:T(1024)}, u32[]{:S(2)}) copy-start(f32[768]{0:T(1024)} %copy-done.12) | copy-start | bytes 9220
  768.2 340.0 %copy-start.15 = (f32[392]{0:T(512)S(1)}, f32[392]{0:T(512)}, u32[]{:S(2)}) copy-start(f32[392]{0:T(512)} %copy-done.14) | copy-start | bytes 4708
  768.2 340.0 %copy-start.17 = (f32[392]{0:T(512)S(1)}, f32[392]{0:T(512)}, u32[]{:S(2)}) copy-start(f32[392]{0:T(512)} %copy-done.16) | copy-start | bytes 4708
  768.2 341.8 %copy-start.3 = (f32[392,768]{1,0:T(8,128)S(1)}, f32[392,768]{1,0:T(8,128)}, u32[]{:S(2)}) copy-start(f32[392,768]{1,0:T(8,128)} %copy-done.2) | copy-start | bytes 3612676
  (1 other events, 0.6 us)
Sparse Core Ops, SparseCore 0:
  90.0 24.6 all-gather.4
  161.5 65.0 all-reduce.22
  618.4 26.8 all-gather.10
  737.2 304.6 all-reduce.26
  1044.3 63.9 all-reduce.24
Sparse Core Ops, SparseCore 1:
  163.6 232.7 all-gather.6
  398.1 199.1 all-gather.8
  749.7 657.2 reduce-scatter.2
  1410.0 648.7 reduce-scatter.4
where the time goes:
time: 2070 us
  waiting for transfers between devices  1600 us (77%)
  blocking collectives  220 us (11%)
  matrix products  145 us (7%)
  other arithmetic  62.9 us (3%)
  local copies, waits for them, and re-layouts  22.2 us (1%)
    reduce_scatter x1, waiting for transfers between devices, body(): lax.psum_scatter(grad_fc2, ('clip', 'head'), scatter_dimension=0, tiled=T...  652 us
    reduce_scatter x1, waiting for transfers between devices, body(): lax.psum_scatter(grad_fc1, ('clip', 'head'), scatter_dimension=1, tiled=T...  218 us
    all_gather x1, waiting for transfers between devices, body(): lax.all_gather(w_fc2, ('clip', 'head'), axis=0, tiled=True)  194 us
    psum x1, waiting for transfers between devices, body(): lax.psum(grad_w_qkv.astype(jnp.bfloat16), 'clip').astype(jnp.float32)  191 us
    all_gather x1, waiting for transfers between devices, body(): lax.all_gather(w_fc1, ('clip', 'head'), axis=1, tiled=True)  167 us
    unnamed x2, blocking collectives  138 us
    psum x1, blocking collectives, body(): lax.psum(grad_qv_bias.astype(jnp.bfloat16), 'clip').astype(jnp.float32)  82.2 us
    psum x1, waiting for transfers between devices, body(): lax.psum(jnp.dot(mixed_low, w_out, preferred_element_type=jnp.float32).as...  63.4 us
  transfers between devices with their start and end apart: 9, of which 9 were waited for; matrix products, arithmetic and copies ran while one was open for 3% of the time, Pallas kernels for 0%

commit v1 on v0

v1 whole, which is shorter than its diff:
```python
from functools import partial

import jax
import jax.numpy as jnp
import numpy as np
from jax import lax
from jax.experimental import pallas as pl
from jax.experimental.pallas import tpu as pltpu
from jax.sharding import PartitionSpec as P

HEAD_DIM = 64
GRID = 14
TOK = 1568
ROWS = 392
D = 768
HEADS_HERE = 3
QCHUNK = 224
CHUNKS = TOK // QCHUNK
UNITS = 384
BLOCKS = 8
epsilon = 1e-06
MESH = pl.DeviceIdType.MESH
VMEM_LIMIT = 60 * 2**20
f32 = jnp.float32
bf16 = jnp.bfloat16
GATHER = (("z", "x", "y"), ("y", "x", "z"), ("y", "z", "x"))
REDUCE = (("x", "z", "y"), ("z", "x", "y"))
RING = ("x", "y", "z")


def dot_nn(left, right):
    return jnp.dot(left, right, preferred_element_type=f32)


def dot_nt(left, right):
    return lax.dot_general(left, right, (((1,), (1,)), ((), ())), preferred_element_type=f32)


def dot_tn(left, right):
    return lax.dot_general(left, right, (((0,), (0,)), ((), ())), preferred_element_type=f32)


class Place:
    def __init__(self):
        clip = lax.axis_index("clip")
        head = lax.axis_index("head")
        self.head = head
        self.index = clip * 4 + head
        self.at = {"x": clip // 8, "y": (head // 2) * 2 + clip % 2, "z": (clip // 2) % 4}
        self.core = head % 2

    def device(self, at, core):
        return {
            "clip": at["x"] * 8 + at["z"] * 2 + at["y"] % 2,
            "head": (at["y"] // 2) * 2 + core,
        }

    def along(self, axis, step):
        at = dict(self.at)
        at[axis] = (at[axis] + step) % 4
        return self.device(at, self.core)

    def partner(self):
        return self.device(self.at, 1 - self.core)

    def across(self):
        at = dict(self.at)
        at["y"] = (at["y"] + 2) % 4
        return self.device(at, 1 - self.core)


def slot_of(axis, value):
    return (value % 2) * 2 + value // 2 if axis == "y" else value


def greet(here):
    barrier = pltpu.get_barrier_semaphore()
    peers = [here.partner(), here.across()]
    peers += [here.along(axis, step) for axis in RING for step in (1, 2, 3)]
    for device in peers:
        pl.semaphore_signal(barrier, inc=1, device_id=device, device_id_type=MESH)
    pl.semaphore_wait(barrier, len(peers))


def remote(src, dst, send, recv, device):
    return pltpu.make_async_remote_copy(
        src_ref=src, dst_ref=dst, send_sem=send, recv_sem=recv, device_id=device, device_id_type=MESH
    )


def ring_total(own, first, second, third):
    return (own + second) + (first + third)


class SmallSum:
    def __init__(self, here, held, arrived, send, recv):
        self.phases = []
        count = 0
        for phase, axis in enumerate(("core", "y", "x", "z")):
            devices = [here.partner()] if axis == "core" else [here.along(axis, k) for k in (1, 2, 3)]
            copies = []
            for device in devices:
                copies.append(
                    remote(held.at[phase], arrived.at[count], send.at[count], recv.at[count], device)
                )
                count += 1
            self.phases.append((copies, list(range(count - len(devices), count))))
        self.held, self.arrived = held, arrived

    def start(self, phase):
        for copy in self.phases[phase][0]:
            copy.start()

    def finish(self, phase):
        copies, slots = self.phases[phase]
        for copy in copies:
            copy.wait_recv()
        total = self.held[phase]
        if len(slots) == 1:
            total = total + self.arrived[slots[0]]
        else:
            total = ring_total(total, *[self.arrived[slot] for slot in slots])
        if phase < 3:
            self.held[phase + 1] = total
        return total

    def drain(self):
        for copies, _ in self.phases:
            for copy in copies:
                copy.wait_send()


def region(fixed):
    return tuple(fixed.get(axis, slice(None)) for axis in ("x", "z", "y"))


def row_mask(cubes, which):
    row = lax.broadcasted_iota(jnp.int32, (ROWS, 196), 0)
    spot = jnp.where(row >= GRID * GRID, row - GRID * GRID, row)
    line = (spot * 1171) >> 14
    cube = (line >> 1) * (GRID // 2) + ((spot - line * GRID) >> 1)
    here = lax.broadcasted_iota(jnp.int32, (ROWS, 196), 1) == cube + which * 49
    return jnp.sum(jnp.where(here, cubes[...].astype(f32), 0.0), axis=1, keepdims=True)


def unit_of(values):
    average = jnp.mean(values, axis=-1, keepdims=True)
    centered = values - average
    inverse = lax.rsqrt(jnp.mean(centered * centered, axis=-1, keepdims=True) + epsilon)
    return centered * inverse, inverse


def unit_back(scaled, unit, inverse):
    return inverse * (
        scaled
        - jnp.mean(scaled, axis=-1, keepdims=True)
        - unit * jnp.mean(scaled * unit, axis=-1, keepdims=True)
    )


MASK, GAIN1, SHIFT1, PROJ, GAIN2, SHIFT2, FC2B = range(7)


def forward_kernel(
    small, cubes, tokens, w_qkv, qv_bias, w_out, w_fc1, w_fc2,
    params, normed_out, qkv_out, lse_out, mixed_keep, mixed_out_keep, mixed_in_out, w_out_all_out, gathered,
    normed, qkv, lse, mixed, mixed_out, mixed_in, w_out_all,
    rows, held, arrived, own_half, their_half, chip_block, block, values_t,
    tok_send, tok_recv, sum_send, sum_recv, half_sem, ff_send, ff_recv, fwd_send, fwd_recv,
    out_send, out_recv, mix_send, mix_recv, local_sem,
):
    here = Place()
    core, head = here.core, here.head
    at = here.at
    mate = head + 1 - 2 * core
    far = (head + 2) % 4
    far_mate = far + 1 - 2 * core

    own_half[0] = w_fc1[...].astype(f32)
    own_half[1] = w_fc2[...].astype(f32)
    column = lax.broadcasted_iota(jnp.int32, (1, D), 1) - here.index * 6
    lines = []
    for k in range(7):
        placed = jnp.zeros((1, D), f32)
        for j in range(6):
            placed = jnp.where(column == j, small[k * 6 + j], placed)
        lines.append(placed)
    held[0, :, 0:D] = jnp.concatenate(lines + [jnp.zeros((1, D), f32)], axis=0)
    line = lax.broadcasted_iota(jnp.int32, (8, UNITS), 0)
    unit = lax.broadcasted_iota(jnp.int32, (8, UNITS), 1) - (here.index % 16) * 24
    shifted = jnp.zeros((8, UNITS), f32)
    for j in range(24):
        shifted = jnp.where(unit == j, small[42 + j], shifted)
    held[0, :, D : D + UNITS] = jnp.where(line == here.index // 16, shifted, 0.0)
    sums = SmallSum(here, held, arrived, sum_send, sum_recv)

    greet(here)
    sums.start(0)

    def tok_copy(way, k):
        lanes = pl.ds(k * 384, 384)
        src = rows.at[far, :, lanes] if way == 2 else tokens.at[:, lanes]
        dst = rows.at[far if way == 2 else head, :, lanes]
        device = here.along("y", 2) if way == 1 else here.partner()
        return remote(src, dst, tok_send.at[way, k], tok_recv.at[way, k], device)

    half_copy = remote(
        own_half.at[:, :, pl.ds(pl.multiple_of((1 - core) * UNITS, UNITS), UNITS)],
        their_half, half_sem.at[0], half_sem.at[1], here.partner(),
    )
    half_copy.start()
    sums.finish(0)
    sums.start(1)
    for way in (1, 0):
        for k in (0, 1):
            tok_copy(way, k).start()

    half_copy.wait_recv()
    mine = pl.ds(pl.multiple_of(core * 24, 8), 24)
    theirs = pl.ds(pl.multiple_of((1 - core) * 24, 8), 24)
    for kind in (0, 1):
        chip_block[kind, mine, :] = own_half[kind, :, pl.ds(pl.multiple_of(core * UNITS, UNITS), UNITS)]
        chip_block[kind, theirs, :] = their_half[kind]
    for part in range(3):
        for kind in (0, 1):
            block[part, kind * 48 : kind * 48 + 48, :] = chip_block[
                kind, :, part * 128 : part * 128 + 128
            ].astype(bf16)

    slots = {axis: slot_of(axis, at[axis]) for axis in RING}
    ours = pl.ds(core * 3, 3)
    block_copy = pltpu.make_async_copy(block, gathered.at[(ours,) + region(slots)], local_sem.at[0])

    def ff_copy(part, phase, step):
        order = GATHER[part]
        spot = gathered.at[(core * 3 + part,) + region({a: slots[a] for a in order[phase:]})]
        return remote(
            block.at[part] if phase == 0 else spot, spot,
            ff_send.at[part, phase, step - 1], ff_recv.at[part, phase, step - 1],
            here.along(order[phase], step),
        )

    def pass_copy(part, step):
        last = GATHER[part][2]
        plane = region({last: slot_of(last, (at[last] + 4 - step) % 4)})
        spot = gathered.at[(core * 3 + part,) + plane]
        return remote(spot, spot, fwd_send.at[part, step], fwd_recv.at[part, step], here.partner())

    def ff_start(part, phase):
        for step in (1, 2, 3):
            ff_copy(part, phase, step).start()

    def ff_on(part, phase):
        for step in (1, 2, 3):
            ff_copy(part, phase, step).wait_recv()
        ff_start(part, phase + 1)
        if phase == 1:
            pass_copy(part, 0).start()

    for part in range(3):
        ff_start(part, 0)
    block_copy.start()

    def out_copy(way):
        src = w_out_all.at[far] if way == 2 else w_out
        dst = w_out_all.at[far if way == 2 else head]
        device = here.along("y", 2) if way == 1 else here.partner()
        return remote(src, dst, out_send.at[way], out_recv.at[way], device)

    out_copy(0).start()
    w_out_all[head] = w_out[...]
    rows[head] = tokens[...]
    sums.finish(1)
    sums.start(2)
    block_copy.wait()
    ff_on(0, 0)
    sums.finish(2)
    sums.start(3)
    for k in (0, 1):
        tok_copy(0, k).wait_recv()
    params[...] = sums.finish(3)

    gain = params[GAIN1 : GAIN1 + 1, 0:D]
    shift = params[SHIFT1 : SHIFT1 + 1, 0:D]
    mask_token = params[MASK : MASK + 1, 0:D]
    biases = qv_bias[...].astype(f32)
    q_bias = biases[0:1, :]
    v_bias = biases[1:2, :]

    def project(half):
        parts = []
        for j in range(2):
            which = half * 2 + j
            masked = row_mask(cubes, which)
            start = jnp.where(masked > 0.5, mask_token, rows[which].astype(f32))
            unit1, _ = unit_of(start)
            parts.append(unit1 * gain + shift)
        normed[half] = jnp.concatenate(parts, axis=0).astype(bf16)

        def some(i, carry):
            part_rows = normed[half, pl.ds(pl.multiple_of(i * 112, 16), 112), :]
            to = pl.ds(pl.multiple_of(half * 784 + i * 112, 16), 112)
            packed = dot_nt(part_rows, w_qkv[...])
            for h in range(HEADS_HERE):
                lanes = slice(h * 64, h * 64 + 64)
                query = packed[:, h * 192 : h * 192 + 64] + q_bias[:, lanes]
                key = packed[:, h * 192 + 64 : h * 192 + 128]
                value = packed[:, h * 192 + 128 : h * 192 + 192] + v_bias[:, lanes]
                qkv[h * 3, to, :] = query.astype(bf16) * bf16(0.125)
                qkv[h * 3 + 1, to, :] = key.astype(bf16)
                qkv[h * 3 + 2, to, :] = value.astype(bf16)
            return carry

        lax.fori_loop(0, 7, some, 0)

    chip_half = head // 2
    project(chip_half)
    ff_on(0, 1)
    for k in (0, 1):
        tok_copy(1, k).wait_recv()
        tok_copy(2, k).start()
    for part in (1, 2):
        ff_on(part, 0)
    out_copy(1).start()
    for k in (0, 1):
        tok_copy(2, k).wait_recv()
    project(1 - chip_half)
    early = [
        pltpu.make_async_copy(normed, normed_out, local_sem.at[1]),
        pltpu.make_async_copy(qkv, qkv_out, local_sem.at[2]),
    ]
    for copy in early:
        copy.start()

    ones_row = (lax.broadcasted_iota(jnp.int32, (16, TOK), 0) == 0).astype(f32)
    for h in range(HEADS_HERE):
        values_t[h] = jnp.concatenate([qkv[h * 3 + 2].astype(f32).T, ones_row], axis=0).astype(bf16)

    def mix_copy(h, way):
        other, device = (
            (mate, here.partner()), (far, here.along("y", 2)), (far_mate, here.across()),
        )[way]
        return remote(
            mixed_out.at[h, other], mixed_in.at[h, head], mix_send.at[h, way], mix_recv.at[h, way], device
        )

    def mix_start(h):
        for j in range(4):
            mixed_out[h, j] = mixed[h, j * ROWS : j * ROWS + ROWS, :].astype(bf16)
        for way in (1, 2, 0):
            mix_copy(h, way).start()
        mixed_in[h, head] = mixed_out[h, head]

    def ff_pass(part, step):
        ff_copy(part, 2, step).wait_recv()
        pass_copy(part, step).start()

    def out_on():
        out_copy(1).wait_recv()
        out_copy(2).start()

    plan = [(CHUNKS - 1, partial(mix_start, 0)), (2 * CHUNKS - 1, partial(mix_start, 1))]
    plan += [(10, out_on), (3, partial(ff_on, 1, 1)), (4, partial(ff_on, 2, 1))]
    plan += [(12 + 3 * k + part, partial(ff_pass, part, k + 1)) for k in range(3) for part in range(3)]

    def attend(i, carry):
        h = i // CHUNKS
        chunk = pl.ds(pl.multiple_of((i % CHUNKS) * QCHUNK, 16), QCHUNK)
        scores = dot_nt(qkv[h * 3 + 1], qkv[h * 3, chunk, :])
        top = jnp.max(scores, axis=0, keepdims=True)
        weights = jnp.exp(scores - top).astype(bf16)
        outcome = dot_nn(values_t[h], weights)
        total = outcome[64:65, :]
        mixed[h, chunk, :] = (outcome[0:64, :] / total).T
        lse[i] = jnp.broadcast_to(top + jnp.log(total), (8, QCHUNK))
        for when, action in plan:
            pl.when(i == when)(action)
        return carry

    lax.fori_loop(0, HEADS_HERE * CHUNKS, attend, 0)

    mix_start(HEADS_HERE - 1)
    out_copy(0).wait_recv()
    out_copy(2).wait_recv()
    late = [
        pltpu.make_async_copy(lse, lse_out, local_sem.at[3]),
        pltpu.make_async_copy(mixed, mixed_keep, local_sem.at[4]),
        pltpu.make_async_copy(mixed_out, mixed_out_keep, local_sem.at[5]),
        pltpu.make_async_copy(w_out_all, w_out_all_out, local_sem.at[6]),
    ]
    for copy in late:
        copy.start()
    for part in range(3):
        for step in range(4):
            pass_copy(part, step).wait_recv()
    for h in range(HEADS_HERE):
        for way in range(3):
            mix_copy(h, way).wait_recv()
    last_copy = pltpu.make_async_copy(mixed_in, mixed_in_out, local_sem.at[7])
    last_copy.start()
    sums.drain()
    half_copy.wait_send()
    for way in range(3):
        out_copy(way).wait_send()
        for k in (0, 1):
            tok_copy(way, k).wait_send()
        for h in range(HEADS_HERE):
            mix_copy(h, way).wait_send()
    for part in range(3):
        for phase in range(3):
            for step in (1, 2, 3):
                ff_copy(part, phase, step).wait_send()
        for step in range(4):
            pass_copy(part, step).wait_send()
    for copy in early + late + [last_copy]:
        copy.wait()


VM = pl.BlockSpec(memory_space=pltpu.VMEM)
SM = pl.BlockSpec(memory_space=pltpu.SMEM)
ANY = pl.BlockSpec(memory_space=pl.ANY)
DMA = pltpu.SemaphoreType.DMA


def shape(dims, kind=bf16):
    return jax.ShapeDtypeStruct(dims, kind)


def forward_call(*args):
    kept = (
        ((2, 784, D), bf16),
        ((9, TOK, 64), bf16),
        ((HEADS_HERE * CHUNKS, 8, QCHUNK), f32),
        ((HEADS_HERE, TOK, 64), f32),
        ((HEADS_HERE, 4, ROWS, 64), bf16),
        ((HEADS_HERE, 4, ROWS, 64), bf16),
        ((4, 192, D), bf16),
    )
    return pl.pallas_call(
        forward_kernel,
        out_shape=(shape((8, D + UNITS), f32),)
        + tuple(shape(*k) for k in kept)
        + (shape((6, 4, 4, 4, 96, 128)),),
        in_specs=[SM] + [VM] * 7,
        out_specs=(VM,) + (ANY,) * 8,
        scratch_shapes=[pltpu.VMEM(*k) for k in kept]
        + [
            pltpu.VMEM((4, ROWS, D), bf16),
            pltpu.VMEM((4, 8, D + UNITS), f32),
            pltpu.VMEM((10, 8, D + UNITS), f32),
            pltpu.VMEM((2, 24, D), f32),
            pltpu.VMEM((2, 24, UNITS), f32),
            pltpu.VMEM((2, 48, UNITS), f32),
            pltpu.VMEM((3, 96, 128), bf16),
            pltpu.VMEM((HEADS_HERE, 80, TOK), bf16),
            DMA((3, 2)), DMA((3, 2)), DMA((10,)), DMA((10,)), DMA((2,)),
            DMA((3, 3, 3)), DMA((3, 3, 3)), DMA((3, 4)), DMA((3, 4)),
            DMA((3,)), DMA((3,)), DMA((HEADS_HERE, 3)), DMA((HEADS_HERE, 3)), DMA((8,)),
        ],
        name="attention_forward",
        compiler_params=pltpu.CompilerParams(
            collective_id=0, has_side_effects=True, vmem_limit_bytes=VMEM_LIMIT
        ),
    )(*args)


SQRT_HALF = 0.7071067811865476
INV_SQRT_2PI = 0.3989422804014327


def feed_forward_kernel(
    cubes, params, tokens, cotangent, mixed_in, w_out_all, weights,
    block_out, grad_middle, grad_branch, grad_mixed, small_grads, reduced_out,
    held, grads, arrived, reduced, normed2, outer, grad_normed2,
    load_sem, pair_send, pair_recv, keep_sem,
):
    here = Place()
    core, head = here.core, here.head

    def load(b):
        chips = pl.ds(b * 8, 8)
        return pltpu.make_async_copy(weights.at[:, chips], held.at[:, chips], load_sem.at[b])

    for b in range(BLOCKS):
        load(b).start()
    barrier = pltpu.get_barrier_semaphore()
    pl.semaphore_signal(barrier, inc=1, device_id=here.partner(), device_id_type=MESH)

    masked = row_mask(cubes, head)
    start = jnp.where(masked > 0.5, params[MASK : MASK + 1, 0:D], tokens[...].astype(f32))
    branch = jnp.zeros((ROWS, D), f32)
    for j in range(4):
        some = jnp.concatenate([mixed_in[h, j] for h in range(HEADS_HERE)], axis=1)
        branch = branch + dot_nn(some, w_out_all[j])
    middle = start + branch + params[PROJ : PROJ + 1, 0:D]
    gain2 = params[GAIN2 : GAIN2 + 1, 0:D]
    unit2, _ = unit_of(middle)
    normed2[...] = (unit2 * gain2 + params[SHIFT2 : SHIFT2 + 1, 0:D]).astype(bf16)
    block_out[...] = middle
    outer[...] = jnp.zeros((ROWS, D), f32)
    grad_normed2[...] = jnp.zeros((ROWS, D), f32)
    pl.semaphore_wait(barrier, 1)
    mates = pl.ds((1 - core) * 3, 3)

    def pair_copy(b):
        chips = pl.ds(b * 8, 8)
        return remote(
            grads.at[mates, chips], arrived.at[:, chips], pair_send.at[b], pair_recv.at[b], here.partner()
        )

    def keep_copy(b):
        chips = pl.ds(b * 8, 8)
        return pltpu.make_async_copy(reduced.at[:, chips], reduced_out.at[:, chips], keep_sem.at[b])

    def add_pair(b):
        chips = pl.ds(b * 8, 8)
        pair_copy(b).wait_recv()
        for part in range(3):
            reduced[part, chips] = (
                grads[core * 3 + part, chips].astype(f32) + arrived[part, chips].astype(f32)
            ).astype(bf16)
        keep_copy(b).start()

    def some_units(b, carry):
        chips = pl.ds(b * 8, 8)
        load(b).wait()

        def weight(kind):
            return jnp.concatenate(
                [
                    held[s, chips, kind * 48 : kind * 48 + 48, :].reshape(UNITS, 128)
                    for s in range(6)
                ],
                axis=1,
            )

        def keep(kind, grad):
            grad = grad.astype(bf16)
            for s in range(6):
                grads[s, chips, kind * 48 : kind * 48 + 48, :] = grad[
                    :, s * 128 : s * 128 + 128
                ].reshape(8, 48, 128)

        inner = dot_nt(normed2[...], weight(0)) + params[pl.ds(b, 1), D : D + UNITS]
        below = 0.5 + 0.5 * lax.erf(inner * SQRT_HALF)
        active = (inner * below).astype(bf16)
        slope = below + inner * (INV_SQRT_2PI * jnp.exp(-0.5 * inner * inner))
        grad_active = dot_nt(cotangent[...], weight(1))
        grad_inner = (grad_active * slope).astype(bf16)
        small_grads[pl.ds(b, 1), D : D + UNITS] = jnp.sum(
            grad_inner.astype(f32), axis=0, keepdims=True
        )
        outer[...] += dot_nn(active, weight(1))
        grad_normed2[...] += dot_nn(grad_inner, weight(0))
        keep(1, dot_tn(active, cotangent[...]))
        keep(0, dot_tn(grad_inner, normed2[...]))
        pair_copy(b).start()

        @pl.when(b > 0)
        def _():
            add_pair(b - 1)

        return carry

    lax.fori_loop(0, BLOCKS, some_units, 0)

    middle = block_out[...]
    block_out[...] = middle + outer[...] + params[FC2B : FC2B + 1, 0:D]
    unit2, inverse2 = unit_of(middle)
    grad_out = cotangent[...].astype(f32)
    back = grad_normed2[...]
    grad_mid = grad_out + unit_back(back * gain2, unit2, inverse2)
    grad_middle[...] = grad_mid
    low = grad_mid.astype(bf16)
    grad_branch[...] = low
    for j in range(4):
        some = dot_nt(low, w_out_all[j]).astype(bf16)
        for h in range(HEADS_HERE):
            grad_mixed[h, j] = some[:, h * 64 : h * 64 + 64]
    sums = [
        jnp.sum(v, axis=0, keepdims=True)
        for v in (grad_mid, back * unit2, back, grad_out)
    ]
    small_grads[:, 0:D] = jnp.concatenate(sums + [jnp.zeros((4, D), f32)], axis=0)
    add_pair(BLOCKS - 1)
    for b in range(BLOCKS):
        pair_copy(b).wait_send()
        keep_copy(b).wait()


def feed_forward_call(*args):
    return pl.pallas_call(
        feed_forward_kernel,
        out_shape=(
            shape((ROWS, D), f32),
            shape((ROWS, D), f32),
            shape((ROWS, D)),
            shape((HEADS_HERE, 4, ROWS, 64)),
            shape((8, D + UNITS), f32),
            shape((3, 64, 96, 128)),
        ),
        in_specs=[VM] * 6 + [ANY],
        out_specs=(VM,) * 5 + (ANY,),
        scratch_shapes=[
            pltpu.VMEM((6, 64, 96, 128), bf16),
            pltpu.VMEM((6, 64, 96, 128), bf16),
            pltpu.VMEM((3, 64, 96, 128), bf16),
            pltpu.VMEM((3, 64, 96, 128), bf16),
            pltpu.VMEM((ROWS, D), bf16),
            pltpu.VMEM((ROWS, D), f32),
            pltpu.VMEM((ROWS, D), f32),
            DMA((BLOCKS,)), DMA((BLOCKS,)), DMA((BLOCKS,)), DMA((BLOCKS,)),
        ],
        name="feed_forward",
        compiler_params=pltpu.CompilerParams(
            collective_id=1, has_side_effects=True, vmem_limit_bytes=VMEM_LIMIT
        ),
    )(*args)


def without(axes, axis):
    return tuple(a for a in axes if a != axis)


def backward_kernel(
    cubes, params, grad_mixed, grad_branch, small_grads, reduced,
    grad_middle_in, tokens_in, normed_in, qkv_in, lse_in, mixed_in, mixed_out_in, w_qkv_in,
    tokens_grad, small_first, small_last, w_grads, w_fc1_grad, w_fc2_grad,
    grad_middle, tokens, normed, qkv, lse, mixed, mixed_out, w_qkv, own_reduced,
    mixed_back, mixed_wide, outer_back, queries, keys_t, grad_q, grad_kv, packed_back,
    branch_in, input_back, pair_out, pair_in, far_out, far_in,
    held, arrived, held_last, arrived_last,
    ff_in0, ff_sum1, ff_in1, ff_sum2, ff_in2, ff_last, ff_mate,
    w_src, w_in, w_z, w_z_in, w_y, w_y_in, w_all, column_sums,
    mix_send, mix_recv, br_send, br_recv, in_send, in_recv, sum_send, sum_recv, last_send, last_recv,
    ff_send, ff_recv, mate_sem, wx_send, wx_recv, wz_send, wz_recv, wy_send, wy_recv, wg_send, wg_recv,
    load_sem,
):
    here = Place()
    core, head, at = here.core, here.head, here.at
    mate = head + 1 - 2 * core
    far = (head + 2) % 4
    far_mate = far + 1 - 2 * core
    slots = {axis: slot_of(axis, at[axis]) for axis in RING}

    def own_share(kind):
        axis = REDUCE[kind][0]
        return reduced.at[(slice(None),) + region({axis: slots[axis]}) + (pl.ds(kind * 48, 48),)]

    pairs = (
        (qkv_in, qkv), (lse_in, lse), (mixed_in, mixed), (tokens_in, tokens), (w_qkv_in, w_qkv),
        (normed_in, normed), (mixed_out_in, mixed_out), (grad_middle_in, grad_middle),
        (own_share(0), own_reduced.at[0]), (own_share(1), own_reduced.at[1]),
    )
    loads = [pltpu.make_async_copy(src, dst, load_sem.at[k]) for k, (src, dst) in enumerate(pairs)]
    for copy in loads:
        copy.start()
    greet(here)

    def mix_copy(h, way):
        other, device = (
            (mate, here.partner()), (far, here.along("y", 2)), (far_mate, here.across()),
        )[way]
        return remote(
            grad_mixed.at[h, other], mixed_back.at[h, head], mix_send.at[h, way], mix_recv.at[h, way], device
        )

    for h in range(HEADS_HERE):
        for way in (1, 2, 0):
            mix_copy(h, way).start()

    def peer_slot(axis, step):
        return slot_of(axis, (at[axis] + step) % 4)

    def ff_left(kind, phase):
        left = ("x", "z", "y")
        for done in REDUCE[kind][:phase]:
            left = without(left, done)
        return left

    def ff_copy(kind, phase, step):
        axis = REDUCE[kind][phase]
        where = tuple(
            peer_slot(axis, step) if a == axis else slice(None) for a in ff_left(kind, phase)
        )
        where = (slice(None),) + where
        if phase == 0:
            src = reduced.at[where + (pl.ds(kind * 48, 48),)]
        else:
            src = (ff_sum1, ff_sum2)[phase - 1].at[(kind,) + where]
        dst = (ff_in0, ff_in1, ff_in2)[phase]
        return remote(
            src, dst.at[kind, step - 1],
            ff_send.at[kind, phase, step - 1], ff_recv.at[kind, phase, step - 1],
            here.along(axis, step),
        )

    def ff_start(kind, phase):
        for step in (1, 2, 3):
            ff_copy(kind, phase, step).start()

    def ff_add(kind, phase):
        axis = REDUCE[kind][phase]
        where = tuple(slots[axis] if a == axis else slice(None) for a in ff_left(kind, phase))
        arrived_in = (ff_in0, ff_in1, ff_in2)[phase]
        for step in (1, 2, 3):
            ff_copy(kind, phase, step).wait_recv()
        if phase == 0:
            loads[8 + kind].wait()

        def some(part):
            if phase == 0:
                own = own_reduced[kind, part]
            else:
                own = (ff_sum1, ff_sum2)[phase - 1][(kind, part) + where]
            return ring_total(
                own.astype(f32), *[arrived_in[kind, k, part].astype(f32) for k in range(3)]
            )

        if phase == 0:
            @pl.loop(0, 3)
            def _(part):
                ff_sum1[kind, part] = some(part).astype(bf16)
        else:
            for part in range(3):
                total = some(part)
                if phase == 1:
                    ff_sum2[kind, part] = total.astype(bf16)
                else:
                    ff_last[kind, :, part * 128 : part * 128 + 128] = total

    for kind in (0, 1):
        ff_start(kind, 0)

    held[0] = small_grads[...]
    sums = SmallSum(here, held, arrived, sum_send, sum_recv)
    sums.start(0)

    beside = dict(at)
    beside["y"] = at["y"] + 1 - 2 * (at["y"] % 2)
    beside = here.device(beside, core)

    def wx_copy(n, step):
        return remote(
            w_src.at[n, (at["x"] + step) % 4], w_in.at[n, step - 1],
            wx_send.at[n, step - 1], wx_recv.at[n, step - 1], here.along("x", step),
        )

    def wz_copy(n, step):
        return remote(
            w_z.at[n], w_z_in.at[n, step - 1], wz_send.at[n, step - 1], wz_recv.at[n, step - 1],
            here.along("z", step),
        )

    def wy_copy(n):
        return remote(w_y.at[n], w_y_in.at[n], wy_send.at[n], wy_recv.at[n], beside)

    def wg_copy(n, step):
        return remote(
            w_all.at[n, at["x"]], w_all.at[n, at["x"]], wg_send.at[n, step - 1], wg_recv.at[n, step - 1],
            here.along("x", step),
        )

    def w_begin(n, grad):
        grad = grad.astype(bf16)
        for s in range(6):
            lanes = slice(s * 128, s * 128 + 128)
            first = s * 192
            for chunk in range(4):
                low, high = max(first, chunk * 288), min(first + 192, chunk * 288 + 288)
                if low < high:
                    w_src[n, chunk, low - chunk * 288 : high - chunk * 288, :] = grad[
                        low - first : high - first, lanes
                    ]
        for step in (1, 2, 3):
            wx_copy(n, step).start()

    def w_second(n):
        for step in (1, 2, 3):
            wx_copy(n, step).wait_recv()
        w_z[n] = ring_total(
            w_src[n, at["x"]].astype(f32), *[w_in[n, k].astype(f32) for k in range(3)]
        ).astype(bf16)
        for step in (1, 2, 3):
            wz_copy(n, step).start()

    def w_third(n):
        for step in (1, 2, 3):
            wz_copy(n, step).wait_recv()
        w_y[n] = ring_total(
            w_z[n].astype(f32), *[w_z_in[n, k].astype(f32) for k in range(3)]
        ).astype(bf16)
        wy_copy(n).start()

    def w_fourth(n):
        wy_copy(n).wait_recv()
        w_all[n, at["x"]] = (w_y[n].astype(f32) + w_y_in[n].astype(f32)).astype(bf16)
        for step in (1, 2, 3):
            wg_copy(n, step).start()

    def w_end(n):
        for step in (1, 2, 3):
            wg_copy(n, step).wait_recv()
        w_grads[n] = w_all[n]

    br_near = remote(grad_branch, branch_in.at[head], br_send.at[0], br_recv.at[0], here.partner())
    br_far = remote(grad_branch, branch_in.at[head], br_send.at[1], br_recv.at[1], here.along("y", 2))
    br_pass = remote(branch_in.at[far], branch_in.at[far], br_send.at[2], br_recv.at[2], here.partner())
    branch_in[head] = grad_branch[...]
    for h in range(HEADS_HERE):
        mixed_back[h, head] = grad_mixed[h, head]

    zeros = jnp.zeros((TOK, 64), bf16)
    loads[0].wait()
    for h in range(HEADS_HERE):
        query = qkv[h * 3]
        queries[h] = jnp.concatenate([zeros, query], axis=1)
        keys_t[h] = qkv[h * 3 + 1].astype(f32).T.astype(bf16)

    def outer_in(h):
        for way in range(3):
            mix_copy(h, way).wait_recv()
        for j in range(4):
            mixed_wide[j * ROWS : j * ROWS + ROWS, :] = mixed_back[h, j].astype(f32)
        outer_back[h] = jnp.concatenate([mixed_wide[...].astype(bf16), zeros], axis=1)

    outer_in(0)
    br_far.start()
    br_near.start()
    for k in (1, 2, 3, 4, 5, 6, 7):
        loads[k].wait()

    def steps(i, plan):
        for when, action in plan:
            pl.when(i == when)(action)

    def branch_on():
        br_far.wait_recv()
        br_pass.start()

    def branch_end():
        br_near.wait_recv()
        br_pass.wait_recv()
        grad = jnp.zeros((192, D), f32)
        for j in range(4):
            some = jnp.concatenate([mixed_out[h, j] for h in range(HEADS_HERE)], axis=1)
            grad = grad + dot_tn(some, branch_in[j])
        w_begin(0, grad)

    def sum_on(phase):
        def action():
            total = sums.finish(phase)
            if phase < 3:
                sums.start(phase + 1)
            else:
                small_first[...] = total
        return action

    def ff_on(part, phase):
        def action():
            ff_add(part, phase)
            if phase < 2:
                ff_start(part, phase + 1)
        return action

    plan = [(1, sum_on(0)), (3, sum_on(1)), (5, sum_on(2)), (7, sum_on(3))]
    plan += [(4, partial(outer_in, 1)), (10, partial(outer_in, 2))]
    plan += [(6, branch_on), (9, branch_end)]
    plan += [(11, partial(w_second, 0)), (13, partial(w_third, 0)), (15, partial(w_fourth, 0)), (17, partial(w_end, 0))]
    plan += [(9, partial(w_second, 1)), (11, partial(w_third, 1)), (13, partial(w_fourth, 1)), (15, partial(w_end, 1))]
    plan += [(16, partial(w_second, 2)), (18, partial(w_third, 2)), (20, partial(w_fourth, 2))]
    plan += [(12, ff_on(0, 0)), (13, ff_on(1, 0))]
    plan += [(16, ff_on(0, 1)), (17, ff_on(1, 1))]
    plan += [(19, ff_on(0, 2)), (20, ff_on(1, 2))]
    lane = lax.broadcasted_iota(jnp.int32, (TOK, 128), 1)

    def attend(i, carry):
        h = i // CHUNKS
        chunk = pl.ds(pl.multiple_of((i % CHUNKS) * QCHUNK, 16), QCHUNK)

        @pl.when(i % CHUNKS == 0)
        def _():
            grad_kv[...] = jnp.zeros((TOK, 128), f32)

        given = outer_back[h, chunk, :]
        given_mixed = given[:, 0:64]
        scores = dot_nt(qkv[h * 3 + 1], qkv[h * 3, chunk, :])
        weights = jnp.exp(scores - lse[i, 0:1, :])
        delta = jnp.sum((given_mixed.astype(f32) * mixed[h, chunk, :]).T, axis=0, keepdims=True)
        grad_weights = dot_nt(qkv[h * 3 + 2], given_mixed)
        grad_scores = (weights * (grad_weights - delta)).astype(bf16)
        grad_kv[...] += dot_nn(weights.astype(bf16), given) + dot_nn(grad_scores, queries[h, chunk, :])
        grad_q[chunk, 0:64] = dot_nn(keys_t[h], grad_scores).T * 0.125

        @pl.when(i % CHUNKS == CHUNKS - 1)
        def _():
            both = grad_kv[...]
            packed_back[:, 0:128] = jnp.where(lane < 64, grad_q[...], both).astype(bf16)
            packed_back[:, 128:192] = both[:, 0:64].astype(bf16)
            column_sums[pl.ds(h, 1), :] = jnp.sum(packed_back[...].astype(f32), axis=0, keepdims=True)
            for half in (0, 1):
                share = dot_nn(
                    packed_back[half * 784 : half * 784 + 784, :],
                    w_qkv[pl.ds(pl.multiple_of(h * 192, 16), 192), :],
                )
                for j in (0, 1):
                    some = share[j * ROWS : j * ROWS + ROWS]

                    @pl.when(h == 0)
                    def _():
                        input_back[half, j] = some

                    @pl.when(h > 0)
                    def _():
                        input_back[half, j] += some

            for n in range(HEADS_HERE):
                @pl.when(h == n)
                def _():
                    w_begin(n + 1, dot_tn(packed_back[...], normed[...]))

        steps(i, plan)
        return carry

    lax.fori_loop(0, HEADS_HERE * CHUNKS, attend, 0)

    chip = head // 2
    pair_out[0] = input_back[1 - chip, 1 - core].astype(bf16)
    pair_out[1] = input_back[chip, 1 - core].astype(bf16)
    pair_copies = [
        remote(pair_out.at[k], pair_in.at[k], in_send.at[k], in_recv.at[k], here.partner()) for k in (0, 1)
    ]
    for copy in pair_copies:
        copy.start()
    far_copy = remote(far_out, far_in, in_send.at[2], in_recv.at[2], here.along("y", 2))
    pair_copies[0].wait_recv()
    far_out[...] = (input_back[1 - chip, core] + pair_in[0].astype(f32)).astype(bf16)
    far_copy.start()
    w_second(3)

    mate_copy = remote(
        ff_last.at[:, pl.ds(pl.multiple_of((1 - core) * 24, 8), 24), :], ff_mate,
        mate_sem.at[0], mate_sem.at[1], here.partner(),
    )
    mate_copy.start()
    w_third(3)

    masked = row_mask(cubes, head)
    start = jnp.where(masked > 0.5, params[MASK : MASK + 1, 0:D], tokens[...].astype(f32))
    unit1, inverse1 = unit_of(start)
    mate_copy.wait_recv()
    for kind, target in ((0, w_fc1_grad), (1, w_fc2_grad)):
        target[:, pl.ds(pl.multiple_of(core * UNITS, UNITS), UNITS)] = ff_last[
            kind, pl.ds(pl.multiple_of(core * 24, 8), 24), :
        ]
        target[:, pl.ds(pl.multiple_of((1 - core) * UNITS, UNITS), UNITS)] = ff_mate[kind]
    w_end(2)
    w_fourth(3)
    pair_copies[1].wait_recv()
    near = input_back[chip, core] + pair_in[1].astype(f32)
    far_copy.wait_recv()
    back = near + far_in[...].astype(f32)
    grad_start = grad_middle[...] + unit_back(
        back * params[GAIN1 : GAIN1 + 1, 0:D], unit1, inverse1
    )
    tokens_grad[...] = jnp.where(masked > 0.5, 0.0, grad_start)
    totals = [
        jnp.sum(v, axis=0, keepdims=True)
        for v in (back * unit1, back, jnp.where(masked > 0.5, grad_start, 0.0))
    ]
    held_last[0, :, 0:384] = jnp.concatenate(
        [v[:, k * 384 : k * 384 + 384] for v in totals for k in (0, 1)] + [jnp.zeros((2, 384), f32)],
        axis=0,
    )
    line = lax.broadcasted_iota(jnp.int32, (8, 192), 0)
    of_query = jnp.concatenate([column_sums[h : h + 1, 0:64] for h in range(HEADS_HERE)], axis=1)
    of_value = jnp.concatenate([column_sums[h : h + 1, 128:192] for h in range(HEADS_HERE)], axis=1)
    held_last[0, :, 384:576] = jnp.where(
        line == 2 * head, of_query, jnp.where(line == 2 * head + 1, of_value, 0.0)
    )
    held_last[0, :, 576:640] = jnp.zeros((8, 64), f32)
    last = SmallSum(here, held_last, arrived_last, last_send, last_recv)
    last.start(0)
    w_end(3)
    for phase in range(3):
        last.finish(phase)
        last.start(phase + 1)
    small_last[...] = last.finish(3)

    sums.drain()
    last.drain()
    for copy in [br_near, br_far, br_pass, far_copy, mate_copy] + pair_copies:
        copy.wait_send()
    for h in range(HEADS_HERE):
        for way in range(3):
            mix_copy(h, way).wait_send()
    for kind in (0, 1):
        for phase in range(3):
            for step in (1, 2, 3):
                ff_copy(kind, phase, step).wait_send()
    for n in range(4):
        for step in (1, 2, 3):
            wx_copy(n, step).wait_send()
            wz_copy(n, step).wait_send()
            wg_copy(n, step).wait_send()
        wy_copy(n).wait_send()


def backward_call(*args):
    loaded = (
        ((ROWS, D), f32),
        ((ROWS, D), bf16),
        ((TOK, D), bf16),
        ((9, TOK, 64), bf16),
        ((HEADS_HERE * CHUNKS, 8, QCHUNK), f32),
        ((HEADS_HERE, TOK, 64), f32),
        ((HEADS_HERE, 4, ROWS, 64), bf16),
        ((576, D), bf16),
    )
    return pl.pallas_call(
        backward_kernel,
        out_shape=(
            shape((ROWS, D), f32),
            shape((8, D + UNITS), f32),
            shape((8, 640), f32),
            shape((4, 4, 288, 128)),
            shape((24, D), f32),
            shape((24, D), f32),
        ),
        in_specs=[VM] * 5 + [ANY] * 9,
        out_specs=(VM,) * 6,
        scratch_shapes=[pltpu.VMEM(*k) for k in loaded]
        + [
            pltpu.VMEM((2, 3, 4, 4, 48, 128), bf16),
            pltpu.VMEM((HEADS_HERE, 4, ROWS, 64), bf16),
            pltpu.VMEM((TOK, 64), f32),
            pltpu.VMEM((HEADS_HERE, TOK, 128), bf16),
            pltpu.VMEM((HEADS_HERE, TOK, 128), bf16),
            pltpu.VMEM((HEADS_HERE, 64, TOK), bf16),
            pltpu.VMEM((TOK, 128), f32),
            pltpu.VMEM((TOK, 128), f32),
            pltpu.VMEM((TOK, 192), bf16),
            pltpu.VMEM((4, ROWS, D), bf16),
            pltpu.VMEM((2, 2, ROWS, D), f32),
            pltpu.VMEM((2, ROWS, D), bf16),
            pltpu.VMEM((2, ROWS, D), bf16),
            pltpu.VMEM((ROWS, D), bf16),
            pltpu.VMEM((ROWS, D), bf16),
            pltpu.VMEM((4, 8, D + UNITS), f32),
            pltpu.VMEM((10, 8, D + UNITS), f32),
            pltpu.VMEM((4, 8, 640), f32),
            pltpu.VMEM((10, 8, 640), f32),
            pltpu.VMEM((2, 3, 3, 4, 4, 48, 128), bf16),
            pltpu.VMEM((2, 3, 4, 4, 48, 128), bf16),
            pltpu.VMEM((2, 3, 3, 4, 48, 128), bf16),
            pltpu.VMEM((2, 3, 4, 48, 128), bf16),
            pltpu.VMEM((2, 3, 3, 48, 128), bf16),
            pltpu.VMEM((2, 48, UNITS), f32),
            pltpu.VMEM((2, 24, UNITS), f32),
            pltpu.VMEM((4, 4, 288, 128), bf16),
            pltpu.VMEM((4, 3, 288, 128), bf16),
            pltpu.VMEM((4, 288, 128), bf16),
            pltpu.VMEM((4, 3, 288, 128), bf16),
            pltpu.VMEM((4, 288, 128), bf16),
            pltpu.VMEM((4, 288, 128), bf16),
            pltpu.VMEM((4, 4, 288, 128), bf16),
            pltpu.VMEM((8, 192), f32),
            DMA((HEADS_HERE, 3)), DMA((HEADS_HERE, 3)), DMA((3,)), DMA((3,)), DMA((3,)), DMA((3,)),
            DMA((10,)), DMA((10,)), DMA((10,)), DMA((10,)),
            DMA((2, 3, 3)), DMA((2, 3, 3)), DMA((2,)),
            DMA((4, 3)), DMA((4, 3)), DMA((4, 3)), DMA((4, 3)), DMA((4,)), DMA((4,)), DMA((4, 3)), DMA((4, 3)),
            DMA((10,)),
        ],
        name="attention_backward",
        compiler_params=pltpu.CompilerParams(
            collective_id=2, has_side_effects=True, vmem_limit_bytes=VMEM_LIMIT
        ),
    )(*args)


def results_kernel(
    block_in, tokens_in, w_grads, w_fc1_in, w_fc2_in, first, last,
    block_out, tokens_grad, mask_grad, gain1_grad, shift1_grad, w_qkv_grad, qv_grad, w_out_grad,
    proj_grad, gain2_grad, shift2_grad, w_fc1_grad, fc1_grad, w_fc2_grad, fc2_grad,
):
    here = Place()
    pairs = (
        (block_in, block_out), (tokens_in, tokens_grad), (w_fc1_in, w_fc1_grad), (w_fc2_in, w_fc2_grad)
    )
    for src, dst in pairs:
        dst[...] = src[...]

    def pick(line, offset, count):
        column = lax.broadcasted_iota(jnp.int32, line.shape, 1) - offset
        spot = lax.broadcasted_iota(jnp.int32, (1, count), 1)
        out = jnp.zeros((1, count), f32)
        for j in range(count):
            one = jnp.sum(jnp.where(column == j, line, 0.0), axis=1, keepdims=True)
            out = jnp.where(spot == j, one, out)
        return out

    index = here.index
    for row, target in ((0, proj_grad), (1, gain2_grad), (2, shift2_grad), (3, fc2_grad)):
        target[...] = pick(first[row : row + 1, 0:D], index * 6, 6)
    fc1_grad[...] = pick(first[pl.ds(index // 16, 1), D : D + UNITS], (index % 16) * 24, 24)
    for k, target in enumerate((gain1_grad, shift1_grad, mask_grad)):
        target[...] = pick(last[pl.ds(2 * k + index // 64, 1), 0:384], (index % 64) * 6, 6)
    for k in (0, 1):
        qv_grad[k : k + 1, :] = last[pl.ds(2 * here.head + k, 1), 384:576]
    for n in range(4):
        for s in range(6):
            lanes = slice(s * 128, s * 128 + 128)
            start = s * 192
            for chunk in range(4):
                low, high = max(start, chunk * 288), min(start + 192, chunk * 288 + 288)
                if low < high:
                    got = w_grads[n, chunk, low - chunk * 288 : high - chunk * 288, :].astype(f32)
                    if n == 0:
                        w_out_grad[low - start : high - start, lanes] = got
                    else:
                        base = (n - 1) * 192 - start
                        w_qkv_grad[base + low : base + high, lanes] = got


def results_call(*args):
    six = shape((1, 6), f32)
    return pl.pallas_call(
        results_kernel,
        out_shape=(
            shape((ROWS, D), f32), shape((ROWS, D), f32), six, six, six, shape((576, D), f32),
            shape((2, 192), f32), shape((192, D), f32), six, six, six,
            shape((24, D), f32), shape((1, 24), f32), shape((24, D), f32), six,
        ),
        in_specs=[VM] * 7,
        out_specs=(VM,) * 15,
        name="results",
        compiler_params=pltpu.CompilerParams(vmem_limit_bytes=VMEM_LIMIT),
    )(*args)


def body(
    tokens, cube_mask, mask_token, norm1_gain, norm1_bias, w_qkv, qv_bias, w_out, proj_bias,
    norm2_gain, norm2_bias, w_fc1, fc1_bias, w_fc2, fc2_bias, cotangent,
):
    small = jnp.concatenate(
        [mask_token, norm1_gain, norm1_bias, proj_bias, norm2_gain, norm2_bias, fc2_bias, fc1_bias]
    ).astype(f32)
    w_qkv_t = w_qkv.T
    params, normed, qkv, lse, mixed, mixed_out, mixed_in, w_out_all, weights = forward_call(
        small, cube_mask, tokens, w_qkv_t, qv_bias, w_out, w_fc1.T, w_fc2,
    )
    block_out, grad_middle, grad_branch, grad_mixed, small_grads, reduced = feed_forward_call(
        cube_mask, params, tokens, cotangent, mixed_in, w_out_all, weights.reshape(6, 64, 96, 128),
    )
    tokens_grad, small_first, small_last, w_grads, w_fc1_grad, w_fc2_grad = backward_call(
        cube_mask, params, grad_mixed, grad_branch, small_grads, reduced.reshape(3, 4, 4, 4, 96, 128),
        grad_middle, tokens, normed.reshape(TOK, D), qkv, lse, mixed, mixed_out, w_qkv_t,
    )
    outs = list(
        results_call(block_out, tokens_grad, w_grads, w_fc1_grad, w_fc2_grad, small_first, small_last)
    )
    for k in (2, 3, 4, 8, 9, 10, 12, 14):
        outs[k] = outs[k].reshape(-1)
    outs[5] = outs[5].T
    outs[11] = outs[11].T
    return tuple(outs)


def solution(mesh):
    every = P(("clip", "head"))
    rows = P(("clip", "head"), None)
    columns = P(None, ("clip", "head"))
    in_specs = (
        rows, P("clip", None), every, every, every, P(None, "head"), P(None, "head"),
        P("head", None), every, every, every, columns, every, rows, every, rows,
    )
    out_specs = (
        rows, rows, every, every, every, P(None, "head"), P(None, "head"), P("head", None),
        every, every, every, columns, every, rows, every,
    )
    return jax.shard_map(body, mesh=mesh, in_specs=in_specs, out_specs=out_specs, check_vma=False)
```

time: 2070 us -> 243 us (0.12)
  waiting for transfers between devices: 1600 us -> 0 us
  Pallas kernels: 0 us -> 236 us
  blocking collectives: 220 us -> 0 us
  matrix products: 145 us -> 0 us
  other arithmetic: 62.9 us -> 0.52 us
    reduce_scatter x2 -> x0, waiting for transfers between devices: 869 us -> none  [the longest x1 652 us: body(): lax.psum_scatter(grad_fc2, ('clip', 'head'), scatter_dimension=0, tiled=T...]
    all_gather x4 -> x0, waiting for transfers between devices: 411 us -> none  [the longest x1 194 us: body(): lax.all_gather(w_fc2, ('clip', 'head'), axis=0, tiled=True)]
    psum x3 -> x0, waiting for transfers between devices: 316 us -> none  [the longest x1 191 us: body(): lax.psum(grad_w_qkv.astype(jnp.bfloat16), 'clip').astype(jnp.float32)]
    pallas_call x0 -> x4, Pallas kernels: none -> 236 us  [the longest x1 122 us: backward_call(): pl.pallas_call(backward_kernel, out_shape=(shape((ROWS, D), f32), shape((...]
    dot_general x18 -> x0, matrix products: 145 us -> none  [the longest x4 25.4 us: contract_last(): lax.dot_general(left, right, (((1,), (1,)), ((), ())), preferred_element_...]
    unnamed x2 -> x0, blocking collectives: 138 us -> none
    psum x1 -> x0, blocking collectives: 82.2 us -> none  [body(): lax.psum(grad_qv_bias.astype(jnp.bfloat16), 'clip').astype(jnp.float32)]
    convert_element_type x17 -> x1, other arithmetic: 37.9 us -> 0.52 us  [body(): small = jnp.concatenate([mask_token, norm1_gain, norm1_bias, proj_bias, n...]
  transfers between devices with their start and end apart: 9 -> 0, of which waited for: 9 -> 0; matrix products, arithmetic and copies ran while one was open for 3% -> 0% of each run, Pallas kernels for 0% -> 0%
where the time goes in v1:
time: 243 us
  Pallas kernels  236 us (97%)
  local copies, waits for them, and re-layouts  5.43 us (2%)
    pallas_call x1, Pallas kernels, backward_call(): pl.pallas_call(backward_kernel, out_shape=(shape((ROWS, D), f32), shape((...  122 us
    pallas_call x1, Pallas kernels, forward_call(): pl.pallas_call(forward_kernel, out_shape=(shape((8, D + UNITS), f32),) +...  83.3 us
    pallas_call x1, Pallas kernels, feed_forward_call(): pl.pallas_call(feed_forward_kernel, out_shape=(shape((ROWS, D), f32), sha...  26 us
    concatenate x1, local copies, waits for them, and re-layouts, body(): jnp.concatenate([mask_token, norm1_gain, norm1_bias, proj_bias, norm2_gai...  5.43 us

profile of v1, /device:TPU:0, one launch (start us, length us, event | category | flops | bytes accessed | tf_op | source)
XLA Modules:
  0.0 243.0 jit_solution(8554711633021370103)
XLA Ops:
  0.6 5.4 %concatenate.3 = bf16[66]{0:T(256)(128)(2,1)S(1)} concatenate(bf16[6]{0:T(256)(128)(2,1)} %param.18, bf16[6]{0:T(256)(128)(2,1)} %param.19, bf16[6]{0:T(256)(128)(2,1)} %param.20, bf16[6]{0:T(256)(128)(2,1)} %param.24, bf16[6]{0:T(256)(128)(2,1)} %param.25, bf16[6]{0:T(256)(128)(2,1)} %param.26, bf16[6]{0:T(256)(128)(2,1)} %param.30, bf16[24]{0:T(256)(128)(2,1)} %param.28), dimensions={0} | concatenate | bytes 264 | tf_op jit(solution)/shard_map/concatenate | solution.py:1145
  6.1 0.5 convert_element_type.3.small
  6.6 83.3 %attention_forward.1 = (f32[8,1152]{1,0:T(8,128)}, bf16[2,784,768]{2,1,0:T(8,128)(2,1)}, bf16[9,1568,64]{2,1,0:T(8,128)(2,1)}, f32[21,8,224]{2,1,0:T(8,128)}, f3...) custom-call(f32[66]{0:T(128)} %convert_element_type.3.small, ...), custom_call_target="tpu_custom_call" | custom-call | tf_op jit(solution)/shard_map/attention_forward/pallas_call | solution.py:439
  89.9 26.0 %feed_forward.1 = (f32[392,768]{1,0:T(8,128)}, f32[392,768]{1,0:T(8,128)}, bf16[392,768]{1,0:T(8,128)(2,1)}, bf16[3,4,392,64]{3,2,1,0:T(8,128)(2,1)}, f32[8,1152...) custom-call(s32[1,196]{1,0:T(1,128)} %cubes.5, f32[8,1152]{1,0:T(8,128)} %get-tuple-element.51.params, ...), custom_call_target="tpu_custom_call" | custom-call | tf_op jit(solution)/shard_map/feed_forward/pallas_call | solution.py:592
  115.9 122.4 %attention_backward.1 = (f32[392,768]{1,0:T(8,128)}, f32[8,1152]{1,0:T(8,128)}, f32[8,640]{1,0:T(8,128)}, bf16[4,4,288,128]{3,2,1,0:T(8,128)(2,1)}, f32[24,768]{1,0:T(8,128)}, /*index=5*/f32[24,768]{1,0:T(8,128)}) custom-call(s32[1,196]{1,0:T(1,128)} %cubes.5, f32[8,1152]{1,0:T(8,128)} %get-tuple-element.51.params, ...), custom_call_target="tpu_custom_call" | custom-call | tf_op jit(solution)/shard_map/attention_backward/pallas_call | solution.py:1020
  238.3 4.6 %results.1 = (f32[392,768]{1,0:T(8,128)}, f32[392,768]{1,0:T(8,128)}, f32[1,6]{1,0:T(1,128)}, f32[1,6]{1,0:T(1,128)}, f32[1,6]{1,0:T(1,128)}, /*index=5*/f32[576...) custom-call(f32[392,768]{1,0:T(8,128)} %get-tuple-element.55.block_i, ...), custom_call_target="tpu_custom_call" | custom-call | tf_op jit(solution)/shard_map/results/pallas_call | solution.py:1127

commit v2 on v1

--- a/solution.py
+++ b/solution.py
@@ -17,13 +17,13 @@
 QCHUNK = 224
 CHUNKS = TOK // QCHUNK
 UNITS = 384
-BLOCKS = 8
+BLOCKS = 4
 epsilon = 1e-06
 MESH = pl.DeviceIdType.MESH
 VMEM_LIMIT = 60 * 2**20
 f32 = jnp.float32
 bf16 = jnp.bfloat16
-GATHER = (("z", "x", "y"), ("y", "x", "z"), ("y", "z", "x"))
+GATHER = (("y", "x", "z"), ("y", "z", "x"))
 REDUCE = (("x", "z", "y"), ("z", "x", "y"))
 RING = ("x", "y", "z")
 
@@ -195,7 +195,6 @@
     sums = SmallSum(here, held, arrived, sum_send, sum_recv)
 
     greet(here)
-    sums.start(0)
 
     def tok_copy(way, k):
         lanes = pl.ds(k * 384, 384)
@@ -209,11 +208,9 @@
         their_half, half_sem.at[0], half_sem.at[1], here.partner(),
     )
     half_copy.start()
+    sums.start(0)
     sums.finish(0)
     sums.start(1)
-    for way in (1, 0):
-        for k in (0, 1):
-            tok_copy(way, k).start()
 
     half_copy.wait_recv()
     mine = pl.ds(pl.multiple_of(core * 24, 8), 24)
@@ -231,35 +228,39 @@
     ours = pl.ds(core * 3, 3)
     block_copy = pltpu.make_async_copy(block, gathered.at[(ours,) + region(slots)], local_sem.at[0])
 
-    def ff_copy(part, phase, step):
-        order = GATHER[part]
-        spot = gathered.at[(core * 3 + part,) + region({a: slots[a] for a in order[phase:]})]
+    def ff_copy(kind, phase, step):
+        order = GATHER[kind]
+        of_kind = pl.ds(kind * 48, 48)
+        spot = gathered.at[(ours,) + region({a: slots[a] for a in order[phase:]}) + (of_kind,)]
         return remote(
-            block.at[part] if phase == 0 else spot, spot,
-            ff_send.at[part, phase, step - 1], ff_recv.at[part, phase, step - 1],
+            block.at[:, of_kind] if phase == 0 else spot, spot,
+            ff_send.at[kind, phase, step - 1], ff_recv.at[kind, phase, step - 1],
             here.along(order[phase], step),
         )
 
-    def pass_copy(part, step):
-        last = GATHER[part][2]
+    def pass_copy(kind, step):
+        last = GATHER[kind][2]
+        of_kind = pl.ds(kind * 48, 48)
         plane = region({last: slot_of(last, (at[last] + 4 - step) % 4)})
-        spot = gathered.at[(core * 3 + part,) + plane]
-        return remote(spot, spot, fwd_send.at[part, step], fwd_recv.at[part, step], here.partner())
-
-    def ff_start(part, phase):
+        spot = gathered.at[(ours,) + plane + (of_kind,)]
+        return remote(spot, spot, fwd_send.at[kind, step], fwd_recv.at[kind, step], here.partner())
+
+    def ff_start(phase):
         for step in (1, 2, 3):
-            ff_copy(part, phase, step).start()
-
-    def ff_on(part, phase):
+            for kind in (0, 1):
+                ff_copy(kind, phase, step).start()
+
+    def ff_on(phase):
         for step in (1, 2, 3):
-            ff_copy(part, phase, step).wait_recv()
-        ff_start(part, phase + 1)
-        if phase == 1:
-            pass_copy(part, 0).start()
-
-    for part in range(3):
-        ff_start(part, 0)
+            for kind in (0, 1):
+                ff_copy(kind, phase, step).wait_recv()
+        ff_start(phase + 1)
+
+    ff_start(0)
     block_copy.start()
+    for way in (1, 0):
+        for k in (0, 1):
+            tok_copy(way, k).start()
 
     def out_copy(way):
         src = w_out_all.at[far] if way == 2 else w_out
@@ -273,7 +274,7 @@
     sums.finish(1)
     sums.start(2)
     block_copy.wait()
-    ff_on(0, 0)
+    ff_on(0)
     sums.finish(2)
     sums.start(3)
     for k in (0, 1):
@@ -297,30 +298,24 @@
             parts.append(unit1 * gain + shift)
         normed[half] = jnp.concatenate(parts, axis=0).astype(bf16)
 
-        def some(i, carry):
-            part_rows = normed[half, pl.ds(pl.multiple_of(i * 112, 16), 112), :]
-            to = pl.ds(pl.multiple_of(half * 784 + i * 112, 16), 112)
-            packed = dot_nt(part_rows, w_qkv[...])
-            for h in range(HEADS_HERE):
-                lanes = slice(h * 64, h * 64 + 64)
-                query = packed[:, h * 192 : h * 192 + 64] + q_bias[:, lanes]
-                key = packed[:, h * 192 + 64 : h * 192 + 128]
-                value = packed[:, h * 192 + 128 : h * 192 + 192] + v_bias[:, lanes]
-                qkv[h * 3, to, :] = query.astype(bf16) * bf16(0.125)
-                qkv[h * 3 + 1, to, :] = key.astype(bf16)
-                qkv[h * 3 + 2, to, :] = value.astype(bf16)
-            return carry
-
-        lax.fori_loop(0, 7, some, 0)
+        to = pl.ds(pl.multiple_of(half * 784, 16), 784)
+        for h in range(HEADS_HERE):
+            packed = dot_nt(normed[half], w_qkv[h * 192 : h * 192 + 192, :])
+            lanes = slice(h * 64, h * 64 + 64)
+            query = packed[:, 0:64] + q_bias[:, lanes]
+            value = packed[:, 128:192] + v_bias[:, lanes]
+            qkv[h * 3, to, :] = query.astype(bf16) * bf16(0.125)
+            qkv[h * 3 + 1, to, :] = packed[:, 64:128].astype(bf16)
+            qkv[h * 3 + 2, to, :] = value.astype(bf16)
 
     chip_half = head // 2
     project(chip_half)
-    ff_on(0, 1)
+    ff_on(1)
+    for kind in (0, 1):
+        pass_copy(kind, 0).start()
     for k in (0, 1):
         tok_copy(1, k).wait_recv()
         tok_copy(2, k).start()
-    for part in (1, 2):
-        ff_on(part, 0)
     out_copy(1).start()
     for k in (0, 1):
         tok_copy(2, k).wait_recv()
@@ -351,35 +346,40 @@
             mix_copy(h, way).start()
         mixed_in[h, head] = mixed_out[h, head]
 
-    def ff_pass(part, step):
-        ff_copy(part, 2, step).wait_recv()
-        pass_copy(part, step).start()
+    def ff_pass(step):
+        for kind in (0, 1):
+            ff_copy(kind, 2, step).wait_recv()
+            pass_copy(kind, step).start()
 
     def out_on():
         out_copy(1).wait_recv()
         out_copy(2).start()
 
-    plan = [(CHUNKS - 1, partial(mix_start, 0)), (2 * CHUNKS - 1, partial(mix_start, 1))]
-    plan += [(10, out_on), (3, partial(ff_on, 1, 1)), (4, partial(ff_on, 2, 1))]
-    plan += [(12 + 3 * k + part, partial(ff_pass, part, k + 1)) for k in range(3) for part in range(3)]
-
-    def attend(i, carry):
-        h = i // CHUNKS
-        chunk = pl.ds(pl.multiple_of((i % CHUNKS) * QCHUNK, 16), QCHUNK)
-        scores = dot_nt(qkv[h * 3 + 1], qkv[h * 3, chunk, :])
-        top = jnp.max(scores, axis=0, keepdims=True)
-        weights = jnp.exp(scores - top).astype(bf16)
-        outcome = dot_nn(values_t[h], weights)
-        total = outcome[64:65, :]
-        mixed[h, chunk, :] = (outcome[0:64, :] / total).T
-        lse[i] = jnp.broadcast_to(top + jnp.log(total), (8, QCHUNK))
-        for when, action in plan:
-            pl.when(i == when)(action)
+    def attend(h, carry):
+        def score(k):
+            scores = dot_nt(qkv[h * 3 + 1], qkv[h * 3, k * QCHUNK : k * QCHUNK + QCHUNK, :])
+            return scores, jnp.max(scores, axis=0, keepdims=True)
+
+        ready = score(0)
+        for k in range(CHUNKS):
+            scores, top = ready
+            if k + 1 < CHUNKS:
+                ready = score(k + 1)
+            weights = jnp.exp(scores - top).astype(bf16)
+            outcome = dot_nn(values_t[h], weights)
+            total = outcome[64:65, :]
+            mixed[h, k * QCHUNK : k * QCHUNK + QCHUNK, :] = (outcome[0:64, :] / total).T
+            lse[h * CHUNKS + k] = jnp.broadcast_to(top + jnp.log(total), (8, QCHUNK))
+        for n in range(HEADS_HERE - 1):
+            pl.when(h == n)(partial(mix_start, n))
+        pl.when(h == 1)(out_on)
         return carry
 
-    lax.fori_loop(0, HEADS_HERE * CHUNKS, attend, 0)
+    lax.fori_loop(0, HEADS_HERE, attend, 0)
 
     mix_start(HEADS_HERE - 1)
+    for step in (1, 2, 3):
+        ff_pass(step)
     out_copy(0).wait_recv()
     out_copy(2).wait_recv()
     late = [
@@ -390,9 +390,9 @@
     ]
     for copy in late:
         copy.start()
-    for part in range(3):
+    for kind in (0, 1):
         for step in range(4):
-            pass_copy(part, step).wait_recv()
+            pass_copy(kind, step).wait_recv()
     for h in range(HEADS_HERE):
         for way in range(3):
             mix_copy(h, way).wait_recv()
@@ -406,12 +406,12 @@
             tok_copy(way, k).wait_send()
         for h in range(HEADS_HERE):
             mix_copy(h, way).wait_send()
-    for part in range(3):
+    for kind in (0, 1):
         for phase in range(3):
             for step in (1, 2, 3):
-                ff_copy(part, phase, step).wait_send()
+                ff_copy(kind, phase, step).wait_send()
         for step in range(4):
-            pass_copy(part, step).wait_send()
+            pass_copy(kind, step).wait_send()
     for copy in early + late + [last_copy]:
         copy.wait()
 
@@ -454,7 +454,7 @@
             pltpu.VMEM((3, 96, 128), bf16),
             pltpu.VMEM((HEADS_HERE, 80, TOK), bf16),
             DMA((3, 2)), DMA((3, 2)), DMA((10,)), DMA((10,)), DMA((2,)),
-            DMA((3, 3, 3)), DMA((3, 3, 3)), DMA((3, 4)), DMA((3, 4)),
+            DMA((2, 3, 3)), DMA((2, 3, 3)), DMA((2, 4)), DMA((2, 4)),
             DMA((3,)), DMA((3,)), DMA((HEADS_HERE, 3)), DMA((HEADS_HERE, 3)), DMA((8,)),
         ],
         name="attention_forward",
@@ -478,7 +478,7 @@
     core, head = here.core, here.head
 
     def load(b):
-        chips = pl.ds(b * 8, 8)
+        chips = pl.ds(b * 16, 16)
         return pltpu.make_async_copy(weights.at[:, chips], held.at[:, chips], load_sem.at[b])
 
     for b in range(BLOCKS):
@@ -503,17 +503,17 @@
     mates = pl.ds((1 - core) * 3, 3)
 
     def pair_copy(b):
-        chips = pl.ds(b * 8, 8)
+        chips = pl.ds(b * 16, 16)
         return remote(
             grads.at[mates, chips], arrived.at[:, chips], pair_send.at[b], pair_recv.at[b], here.partner()
         )
 
     def keep_copy(b):
-        chips = pl.ds(b * 8, 8)
+        chips = pl.ds(b * 16, 16)
         return pltpu.make_async_copy(reduced.at[:, chips], reduced_out.at[:, chips], keep_sem.at[b])
 
     def add_pair(b):
-        chips = pl.ds(b * 8, 8)
+        chips = pl.ds(b * 16, 16)
         pair_copy(b).wait_recv()
         for part in range(3):
             reduced[part, chips] = (
@@ -522,13 +522,13 @@
         keep_copy(b).start()
 
     def some_units(b, carry):
-        chips = pl.ds(b * 8, 8)
         load(b).wait()
+        chips = pl.ds(b * 16, 16)
 
         def weight(kind):
             return jnp.concatenate(
                 [
-                    held[s, chips, kind * 48 : kind * 48 + 48, :].reshape(UNITS, 128)
+                    held[s, chips, kind * 48 : kind * 48 + 48, :].reshape(2 * UNITS, 128)
                     for s in range(6)
                 ],
                 axis=1,
@@ -539,17 +539,20 @@
             for s in range(6):
                 grads[s, chips, kind * 48 : kind * 48 + 48, :] = grad[
                     :, s * 128 : s * 128 + 128
-                ].reshape(8, 48, 128)
-
-        inner = dot_nt(normed2[...], weight(0)) + params[pl.ds(b, 1), D : D + UNITS]
+                ].reshape(16, 48, 128)
+
+        bias = jnp.concatenate(
+            [params[pl.ds(2 * b + k, 1), D : D + UNITS] for k in (0, 1)], axis=1
+        )
+        inner = dot_nt(normed2[...], weight(0)) + bias
         below = 0.5 + 0.5 * lax.erf(inner * SQRT_HALF)
         active = (inner * below).astype(bf16)
         slope = below + inner * (INV_SQRT_2PI * jnp.exp(-0.5 * inner * inner))
         grad_active = dot_nt(cotangent[...], weight(1))
         grad_inner = (grad_active * slope).astype(bf16)
-        small_grads[pl.ds(b, 1), D : D + UNITS] = jnp.sum(
-            grad_inner.astype(f32), axis=0, keepdims=True
-        )
+        bias_grad = jnp.sum(grad_inner.astype(f32), axis=0, keepdims=True)
+        for k in (0, 1):
+            small_grads[pl.ds(2 * b + k, 1), D : D + UNITS] = bias_grad[:, k * UNITS : k * UNITS + UNITS]
         outer[...] += dot_nn(active, weight(1))
         grad_normed2[...] += dot_nn(grad_inner, weight(0))
         keep(1, dot_tn(active, cotangent[...]))
@@ -740,25 +743,30 @@
     beside["y"] = at["y"] + 1 - 2 * (at["y"] % 2)
     beside = here.device(beside, core)
 
+    def first_axis(n):
+        return "xz"[n % 2]
+
     def wx_copy(n, step):
+        axis = first_axis(n)
         return remote(
-            w_src.at[n, (at["x"] + step) % 4], w_in.at[n, step - 1],
-            wx_send.at[n, step - 1], wx_recv.at[n, step - 1], here.along("x", step),
+            w_src.at[n, (at[axis] + step) % 4], w_in.at[n, step - 1],
+            wx_send.at[n, step - 1], wx_recv.at[n, step - 1], here.along(axis, step),
         )
 
     def wz_copy(n, step):
         return remote(
             w_z.at[n], w_z_in.at[n, step - 1], wz_send.at[n, step - 1], wz_recv.at[n, step - 1],
-            here.along("z", step),
+            here.along(first_axis(n + 1), step),
         )
 
     def wy_copy(n):
         return remote(w_y.at[n], w_y_in.at[n], wy_send.at[n], wy_recv.at[n], beside)
 
     def wg_copy(n, step):
+        axis = first_axis(n)
+        spot = w_all.at[n, at[axis]]
         return remote(
-            w_all.at[n, at["x"]], w_all.at[n, at["x"]], wg_send.at[n, step - 1], wg_recv.at[n, step - 1],
-            here.along("x", step),
+            spot, spot, wg_send.at[n, step - 1], wg_recv.at[n, step - 1], here.along(axis, step)
         )
 
     def w_begin(n, grad):
@@ -779,7 +787,7 @@
         for step in (1, 2, 3):
             wx_copy(n, step).wait_recv()
         w_z[n] = ring_total(
-            w_src[n, at["x"]].astype(f32), *[w_in[n, k].astype(f32) for k in range(3)]
+            w_src[n, at[first_axis(n)]].astype(f32), *[w_in[n, k].astype(f32) for k in range(3)]
         ).astype(bf16)
         for step in (1, 2, 3):
             wz_copy(n, step).start()
@@ -794,7 +802,7 @@
 
     def w_fourth(n):
         wy_copy(n).wait_recv()
-        w_all[n, at["x"]] = (w_y[n].astype(f32) + w_y_in[n].astype(f32)).astype(bf16)
+        w_all[n, at[first_axis(n)]] = (w_y[n].astype(f32) + w_y_in[n].astype(f32)).astype(bf16)
         for step in (1, 2, 3):
             wg_copy(n, step).start()
 
@@ -829,10 +837,6 @@
     br_near.start()
     for k in (1, 2, 3, 4, 5, 6, 7):
         loads[k].wait()
-
-    def steps(i, plan):
-        for when, action in plan:
-            pl.when(i == when)(action)
 
     def branch_on():
         br_far.wait_recv()
@@ -848,114 +852,114 @@
         w_begin(0, grad)
 
     def sum_on(phase):
-        def action():
-            total = sums.finish(phase)
-            if phase < 3:
-                sums.start(phase + 1)
+        total = sums.finish(phase)
+        if phase < 3:
+            sums.start(phase + 1)
+        else:
+            small_first[...] = total
+
+    def ff_on(phase):
+        for kind in (0, 1):
+            ff_add(kind, phase)
+            if phase < 2:
+                ff_start(kind, phase + 1)
+
+    chip = head // 2
+    lane = lax.broadcasted_iota(jnp.int32, (TOK, 128), 1)
+
+    def attend(h, carry):
+        def score(k):
+            chunk = slice(k * QCHUNK, k * QCHUNK + QCHUNK)
+            scores = dot_nt(qkv[h * 3 + 1], qkv[h * 3, chunk, :])
+            return scores, dot_nt(qkv[h * 3 + 2], outer_back[h, chunk, 0:64])
+
+        ready = score(0)
+        for k in range(CHUNKS):
+            chunk = slice(k * QCHUNK, k * QCHUNK + QCHUNK)
+            scores, grad_weights = ready
+            if k + 1 < CHUNKS:
+                ready = score(k + 1)
+            given = outer_back[h, chunk, :]
+            weights = jnp.exp(scores - lse[h * CHUNKS + k, 0:1, :])
+            delta = jnp.sum(
+                (given[:, 0:64].astype(f32) * mixed[h, chunk, :]).T, axis=0, keepdims=True
+            )
+            grad_scores = (weights * (grad_weights - delta)).astype(bf16)
+            share = dot_nn(weights.astype(bf16), given) + dot_nn(grad_scores, queries[h, chunk, :])
+            if k == 0:
+                grad_kv[...] = share
             else:
-                small_first[...] = total
-        return action
-
-    def ff_on(part, phase):
-        def action():
-            ff_add(part, phase)
-            if phase < 2:
-                ff_start(part, phase + 1)
-        return action
-
-    plan = [(1, sum_on(0)), (3, sum_on(1)), (5, sum_on(2)), (7, sum_on(3))]
-    plan += [(4, partial(outer_in, 1)), (10, partial(outer_in, 2))]
-    plan += [(6, branch_on), (9, branch_end)]
-    plan += [(11, partial(w_second, 0)), (13, partial(w_third, 0)), (15, partial(w_fourth, 0)), (17, partial(w_end, 0))]
-    plan += [(9, partial(w_second, 1)), (11, partial(w_third, 1)), (13, partial(w_fourth, 1)), (15, partial(w_end, 1))]
-    plan += [(16, partial(w_second, 2)), (18, partial(w_third, 2)), (20, partial(w_fourth, 2))]
-    plan += [(12, ff_on(0, 0)), (13, ff_on(1, 0))]
-    plan += [(16, ff_on(0, 1)), (17, ff_on(1, 1))]
-    plan += [(19, ff_on(0, 2)), (20, ff_on(1, 2))]
-    lane = lax.broadcasted_iota(jnp.int32, (TOK, 128), 1)
-
-    def attend(i, carry):
-        h = i // CHUNKS
-        chunk = pl.ds(pl.multiple_of((i % CHUNKS) * QCHUNK, 16), QCHUNK)
-
-        @pl.when(i % CHUNKS == 0)
+                grad_kv[...] += share
+            grad_q[chunk, 0:64] = dot_nn(keys_t[h], grad_scores).T * 0.125
+
+        both = grad_kv[...]
+        packed_back[:, 0:128] = jnp.where(lane < 64, grad_q[...], both).astype(bf16)
+        packed_back[:, 128:192] = both[:, 0:64].astype(bf16)
+        for half in (1 - chip, chip):
+            share = dot_nn(
+                packed_back[pl.ds(pl.multiple_of(half * 784, 16), 784), :],
+                w_qkv[pl.ds(pl.multiple_of(h * 192, 16), 192), :],
+            )
+            for j in (0, 1):
+                some = share[j * ROWS : j * ROWS + ROWS]
+
+                @pl.when(h == 0)
+                def _():
+                    input_back[half, j] = some
+
+                @pl.when(h > 0)
+                def _():
+                    input_back[half, j] += some
+
+            k = 0 if half is not chip else 1
+            pl.when(h == HEADS_HERE - 1)(partial(pair_start, k, half))
+        column_sums[pl.ds(h, 1), :] = jnp.sum(packed_back[...].astype(f32), axis=0, keepdims=True)
+        w_grad = dot_tn(packed_back[...], normed[...])
+        for n in range(HEADS_HERE):
+            pl.when(h == n)(partial(w_begin, n + 1, w_grad))
+
+        @pl.when(h == 0)
         def _():
-            grad_kv[...] = jnp.zeros((TOK, 128), f32)
-
-        given = outer_back[h, chunk, :]
-        given_mixed = given[:, 0:64]
-        scores = dot_nt(qkv[h * 3 + 1], qkv[h * 3, chunk, :])
-        weights = jnp.exp(scores - lse[i, 0:1, :])
-        delta = jnp.sum((given_mixed.astype(f32) * mixed[h, chunk, :]).T, axis=0, keepdims=True)
-        grad_weights = dot_nt(qkv[h * 3 + 2], given_mixed)
-        grad_scores = (weights * (grad_weights - delta)).astype(bf16)
-        grad_kv[...] += dot_nn(weights.astype(bf16), given) + dot_nn(grad_scores, queries[h, chunk, :])
-        grad_q[chunk, 0:64] = dot_nn(keys_t[h], grad_scores).T * 0.125
-
-        @pl.when(i % CHUNKS == CHUNKS - 1)
+            outer_in(1)
+            sum_on(0)
+
+        @pl.when(h == 1)
         def _():
-            both = grad_kv[...]
-            packed_back[:, 0:128] = jnp.where(lane < 64, grad_q[...], both).astype(bf16)
-            packed_back[:, 128:192] = both[:, 0:64].astype(bf16)
-            column_sums[pl.ds(h, 1), :] = jnp.sum(packed_back[...].astype(f32), axis=0, keepdims=True)
-            for half in (0, 1):
-                share = dot_nn(
-                    packed_back[half * 784 : half * 784 + 784, :],
-                    w_qkv[pl.ds(pl.multiple_of(h * 192, 16), 192), :],
-                )
-                for j in (0, 1):
-                    some = share[j * ROWS : j * ROWS + ROWS]
-
-                    @pl.when(h == 0)
-                    def _():
-                        input_back[half, j] = some
-
-                    @pl.when(h > 0)
-                    def _():
-                        input_back[half, j] += some
-
-            for n in range(HEADS_HERE):
-                @pl.when(h == n)
-                def _():
-                    w_begin(n + 1, dot_tn(packed_back[...], normed[...]))
-
-        steps(i, plan)
+            outer_in(2)
+            sum_on(1)
+            branch_on()
+
         return carry
 
-    lax.fori_loop(0, HEADS_HERE * CHUNKS, attend, 0)
-
-    chip = head // 2
-    pair_out[0] = input_back[1 - chip, 1 - core].astype(bf16)
-    pair_out[1] = input_back[chip, 1 - core].astype(bf16)
     pair_copies = [
         remote(pair_out.at[k], pair_in.at[k], in_send.at[k], in_recv.at[k], here.partner()) for k in (0, 1)
     ]
-    for copy in pair_copies:
-        copy.start()
     far_copy = remote(far_out, far_in, in_send.at[2], in_recv.at[2], here.along("y", 2))
+
+    def pair_start(k, half):
+        pair_out[k] = input_back[half, 1 - core].astype(bf16)
+        pair_copies[k].start()
+
+    lax.fori_loop(0, HEADS_HERE, attend, 0)
+
     pair_copies[0].wait_recv()
     far_out[...] = (input_back[1 - chip, core] + pair_in[0].astype(f32)).astype(bf16)
     far_copy.start()
+    ff_on(0)
+    branch_end()
+    w_second(1)
+    w_second(2)
+    sum_on(2)
+    ff_on(1)
     w_second(3)
-
-    mate_copy = remote(
-        ff_last.at[:, pl.ds(pl.multiple_of((1 - core) * 24, 8), 24), :], ff_mate,
-        mate_sem.at[0], mate_sem.at[1], here.partner(),
-    )
-    mate_copy.start()
-    w_third(3)
+    w_third(1)
+    w_third(2)
+    sum_on(3)
+    w_second(0)
 
     masked = row_mask(cubes, head)
     start = jnp.where(masked > 0.5, params[MASK : MASK + 1, 0:D], tokens[...].astype(f32))
     unit1, inverse1 = unit_of(start)
-    mate_copy.wait_recv()
-    for kind, target in ((0, w_fc1_grad), (1, w_fc2_grad)):
-        target[:, pl.ds(pl.multiple_of(core * UNITS, UNITS), UNITS)] = ff_last[
-            kind, pl.ds(pl.multiple_of(core * 24, 8), 24), :
-        ]
-        target[:, pl.ds(pl.multiple_of((1 - core) * UNITS, UNITS), UNITS)] = ff_mate[kind]
-    w_end(2)
-    w_fourth(3)
     pair_copies[1].wait_recv()
     near = input_back[chip, core] + pair_in[1].astype(f32)
     far_copy.wait_recv()
@@ -981,11 +985,35 @@
     held_last[0, :, 576:640] = jnp.zeros((8, 64), f32)
     last = SmallSum(here, held_last, arrived_last, last_send, last_recv)
     last.start(0)
+    w_third(3)
+    last.finish(0)
+    last.start(1)
+    w_fourth(1)
+    w_fourth(2)
+    ff_on(2)
+    mate_copy = remote(
+        ff_last.at[:, pl.ds(pl.multiple_of((1 - core) * 24, 8), 24), :], ff_mate,
+        mate_sem.at[0], mate_sem.at[1], here.partner(),
+    )
+    mate_copy.start()
+    last.finish(1)
+    last.start(2)
+    w_third(0)
+    w_fourth(3)
+    last.finish(2)
+    last.start(3)
+    w_fourth(0)
+    mate_copy.wait_recv()
+    for kind, target in ((0, w_fc1_grad), (1, w_fc2_grad)):
+        target[:, pl.ds(pl.multiple_of(core * UNITS, UNITS), UNITS)] = ff_last[
+            kind, pl.ds(pl.multiple_of(core * 24, 8), 24), :
+        ]
+        target[:, pl.ds(pl.multiple_of((1 - core) * UNITS, UNITS), UNITS)] = ff_mate[kind]
+    w_end(1)
+    w_end(2)
+    small_last[...] = last.finish(3)
     w_end(3)
-    for phase in range(3):
-        last.finish(phase)
-        last.start(phase + 1)
-    small_last[...] = last.finish(3)
+    w_end(0)
 
     sums.drain()
     last.drain()

time: 243 us -> 190 us (0.78)
  Pallas kernels: 236 us -> 182 us
    pallas_call x1, Pallas kernels: 122 us -> 88.5 us  [backward_call(): pl.pallas_call(backward_kernel, out_shape=(shape((ROWS, D), f32), shape((...]
    pallas_call x1, Pallas kernels: 83.3 us -> 64.6 us  [forward_call(): pl.pallas_call(forward_kernel, out_shape=(shape((8, D + UNITS), f32),) +...]
where the time goes in v2:
time: 190 us; the launch traced here: 189 us
  Pallas kernels  182 us (96%)
  local copies, waits for them, and re-layouts  5.43 us (3%)
    pallas_call x1, Pallas kernels, backward_call(): pl.pallas_call(backward_kernel, out_shape=(shape((ROWS, D), f32), shape((...  88.5 us
    pallas_call x1, Pallas kernels, forward_call(): pl.pallas_call(forward_kernel, out_shape=(shape((8, D + UNITS), f32),) +...  64.6 us
    pallas_call x1, Pallas kernels, feed_forward_call(): pl.pallas_call(feed_forward_kernel, out_shape=(shape((ROWS, D), f32), sha...  24.8 us
    concatenate x1, local copies, waits for them, and re-layouts, body(): jnp.concatenate([mask_token, norm1_gain, norm1_bias, proj_bias, norm2_gai...  5.43 us
    pallas_call x1, Pallas kernels, results_call(): pl.pallas_call(results_kernel, out_shape=(shape((ROWS, D), f32), shape((R...  4.56 us

profile of v2, /device:TPU:0, one launch (start us, length us, event | category | flops | bytes accessed | tf_op | source)
XLA Modules:
  0.0 189.3 jit_solution(10642056674535284041)
XLA Ops:
  0.6 5.4 %concatenate.3 = bf16[66]{0:T(256)(128)(2,1)S(1)} concatenate(bf16[6]{0:T(256)(128)(2,1)} %param.18, bf16[6]{0:T(256)(128)(2,1)} %param.19, bf16[6]{0:T(256)(128)(2,1)} %param.20, bf16[6]{0:T(256)(128)(2,1)} %param.24, bf16[6]{0:T(256)(128)(2,1)} %param.25, bf16[6]{0:T(256)(128)(2,1)} %param.26, bf16[6]{0:T(256)(128)(2,1)} %param.30, bf16[24]{0:T(256)(128)(2,1)} %param.28), dimensions={0} | concatenate | bytes 264 | tf_op jit(solution)/shard_map/concatenate | solution.py:1173
  6.1 0.5 convert_element_type.3.small
  6.6 64.6 %attention_forward.1 = (f32[8,1152]{1,0:T(8,128)}, bf16[2,784,768]{2,1,0:T(8,128)(2,1)}, bf16[9,1568,64]{2,1,0:T(8,128)(2,1)}, f32[21,8,224]{2,1,0:T(8,128)}, f3...) custom-call(f32[66]{0:T(128)} %convert_element_type.3.small, ...), custom_call_target="tpu_custom_call" | custom-call | tf_op jit(solution)/shard_map/attention_forward/pallas_call | solution.py:439
  71.2 24.8 %feed_forward.1 = (f32[392,768]{1,0:T(8,128)}, f32[392,768]{1,0:T(8,128)}, bf16[392,768]{1,0:T(8,128)(2,1)}, bf16[3,4,392,64]{3,2,1,0:T(8,128)(2,1)}, f32[8,1152...) custom-call(s32[1,196]{1,0:T(1,128)} %cubes.5, f32[8,1152]{1,0:T(8,128)} %get-tuple-element.51.params, ...), custom_call_target="tpu_custom_call" | custom-call | tf_op jit(solution)/shard_map/feed_forward/pallas_call | solution.py:595
  96.0 88.5 %attention_backward.1 = (f32[392,768]{1,0:T(8,128)}, f32[8,1152]{1,0:T(8,128)}, f32[8,640]{1,0:T(8,128)}, bf16[4,4,288,128]{3,2,1,0:T(8,128)(2,1)}, f32[24,768]{1,0:T(8,128)}, /*index=5*/f32[24,768]{1,0:T(8,128)}) custom-call(s32[1,196]{1,0:T(1,128)} %cubes.5, f32[8,1152]{1,0:T(8,128)} %get-tuple-element.51.params, ...), custom_call_target="tpu_custom_call" | custom-call | tf_op jit(solution)/shard_map/attention_backward/pallas_call | solution.py:1048
  184.6 4.6 %results.1 = (f32[392,768]{1,0:T(8,128)}, f32[392,768]{1,0:T(8,128)}, f32[1,6]{1,0:T(1,128)}, f32[1,6]{1,0:T(1,128)}, f32[1,6]{1,0:T(1,128)}, /*index=5*/f32[576...) custom-call(f32[392,768]{1,0:T(8,128)} %get-tuple-element.55.block_i, ...), custom_call_target="tpu_custom_call" | custom-call | tf_op jit(solution)/shard_map/results/pallas_call | solution.py:1155

commit v3 on v2

--- a/solution.py
+++ b/solution.py
@@ -162,9 +162,10 @@
 
 
 def forward_kernel(
-    small, cubes, tokens, w_qkv, qv_bias, w_out, w_fc1, w_fc2,
-    params, normed_out, qkv_out, lse_out, mixed_keep, mixed_out_keep, mixed_in_out, w_out_all_out, gathered,
-    normed, qkv, lse, mixed, mixed_out, mixed_in, w_out_all,
+    small, fc1_bias, cubes, tokens, w_qkv, qv_bias, w_out, w_fc1, w_fc2,
+    params, normed_out, qkv_out, lse_out, mixed_keep, mixed_out_keep, mixed_in_out, w_out_all_out,
+    w_last_all_out, gathered,
+    normed, qkv, lse, mixed, mixed_out, mixed_in, w_out_all, w_last_all,
     rows, held, arrived, own_half, their_half, chip_block, block, values_t,
     tok_send, tok_recv, sum_send, sum_recv, half_sem, ff_send, ff_recv, fwd_send, fwd_recv,
     out_send, out_recv, mix_send, mix_recv, local_sem,
@@ -178,19 +179,18 @@
 
     own_half[0] = w_fc1[...].astype(f32)
     own_half[1] = w_fc2[...].astype(f32)
-    column = lax.broadcasted_iota(jnp.int32, (1, D), 1) - here.index * 6
-    lines = []
-    for k in range(7):
-        placed = jnp.zeros((1, D), f32)
-        for j in range(6):
-            placed = jnp.where(column == j, small[k * 6 + j], placed)
-        lines.append(placed)
-    held[0, :, 0:D] = jnp.concatenate(lines + [jnp.zeros((1, D), f32)], axis=0)
+    column = lax.broadcasted_iota(jnp.int32, (8, D), 1) - here.index * 6
+    own_small = small[...].astype(f32)
+    placed = jnp.zeros((8, D), f32)
+    for j in range(6):
+        placed = jnp.where(column == j, own_small[:, j : j + 1], placed)
+    held[0, :, 0:D] = placed
     line = lax.broadcasted_iota(jnp.int32, (8, UNITS), 0)
     unit = lax.broadcasted_iota(jnp.int32, (8, UNITS), 1) - (here.index % 16) * 24
     shifted = jnp.zeros((8, UNITS), f32)
+    own_bias = fc1_bias[...].astype(f32)
     for j in range(24):
-        shifted = jnp.where(unit == j, small[42 + j], shifted)
+        shifted = jnp.where(unit == j, own_bias[:, j : j + 1], shifted)
     held[0, :, D : D + UNITS] = jnp.where(line == here.index // 16, shifted, 0.0)
     sums = SmallSum(here, held, arrived, sum_send, sum_recv)
 
@@ -262,14 +262,20 @@
         for k in (0, 1):
             tok_copy(way, k).start()
 
-    def out_copy(way):
-        src = w_out_all.at[far] if way == 2 else w_out
-        dst = w_out_all.at[far if way == 2 else head]
+    last_rows = pl.ds(384, 192)
+
+    def out_copy(way, k):
+        own = (w_out, w_qkv.at[last_rows])[k]
+        every = (w_out_all, w_last_all)[k]
+        src = every.at[far] if way == 2 else own
+        dst = every.at[far if way == 2 else head]
         device = here.along("y", 2) if way == 1 else here.partner()
-        return remote(src, dst, out_send.at[way], out_recv.at[way], device)
-
-    out_copy(0).start()
+        return remote(src, dst, out_send.at[way, k], out_recv.at[way, k], device)
+
+    for k in (0, 1):
+        out_copy(0, k).start()
     w_out_all[head] = w_out[...]
+    w_last_all[head] = w_qkv[384:576, :]
     rows[head] = tokens[...]
     sums.finish(1)
     sums.start(2)
@@ -316,7 +322,8 @@
     for k in (0, 1):
         tok_copy(1, k).wait_recv()
         tok_copy(2, k).start()
-    out_copy(1).start()
+    for k in (0, 1):
+        out_copy(1, k).start()
     for k in (0, 1):
         tok_copy(2, k).wait_recv()
     project(1 - chip_half)
@@ -352,8 +359,9 @@
             pass_copy(kind, step).start()
 
     def out_on():
-        out_copy(1).wait_recv()
-        out_copy(2).start()
+        for k in (0, 1):
+            out_copy(1, k).wait_recv()
+            out_copy(2, k).start()
 
     def attend(h, carry):
         def score(k):
@@ -380,13 +388,15 @@
     mix_start(HEADS_HERE - 1)
     for step in (1, 2, 3):
         ff_pass(step)
-    out_copy(0).wait_recv()
-    out_copy(2).wait_recv()
+    for k in (0, 1):
+        out_copy(0, k).wait_recv()
+        out_copy(2, k).wait_recv()
     late = [
         pltpu.make_async_copy(lse, lse_out, local_sem.at[3]),
         pltpu.make_async_copy(mixed, mixed_keep, local_sem.at[4]),
         pltpu.make_async_copy(mixed_out, mixed_out_keep, local_sem.at[5]),
         pltpu.make_async_copy(w_out_all, w_out_all_out, local_sem.at[6]),
+        pltpu.make_async_copy(w_last_all, w_last_all_out, local_sem.at[8]),
     ]
     for copy in late:
         copy.start()
@@ -401,8 +411,8 @@
     sums.drain()
     half_copy.wait_send()
     for way in range(3):
-        out_copy(way).wait_send()
         for k in (0, 1):
+            out_copy(way, k).wait_send()
             tok_copy(way, k).wait_send()
         for h in range(HEADS_HERE):
             mix_copy(h, way).wait_send()
@@ -417,7 +427,6 @@
 
 
 VM = pl.BlockSpec(memory_space=pltpu.VMEM)
-SM = pl.BlockSpec(memory_space=pltpu.SMEM)
 ANY = pl.BlockSpec(memory_space=pl.ANY)
 DMA = pltpu.SemaphoreType.DMA
 
@@ -435,14 +444,15 @@
         ((HEADS_HERE, 4, ROWS, 64), bf16),
         ((HEADS_HERE, 4, ROWS, 64), bf16),
         ((4, 192, D), bf16),
+        ((4, 192, D), bf16),
     )
     return pl.pallas_call(
         forward_kernel,
         out_shape=(shape((8, D + UNITS), f32),)
         + tuple(shape(*k) for k in kept)
         + (shape((6, 4, 4, 4, 96, 128)),),
-        in_specs=[SM] + [VM] * 7,
-        out_specs=(VM,) + (ANY,) * 8,
+        in_specs=[VM] * 9,
+        out_specs=(VM,) + (ANY,) * 9,
         scratch_shapes=[pltpu.VMEM(*k) for k in kept]
         + [
             pltpu.VMEM((4, ROWS, D), bf16),
@@ -455,7 +465,7 @@
             pltpu.VMEM((HEADS_HERE, 80, TOK), bf16),
             DMA((3, 2)), DMA((3, 2)), DMA((10,)), DMA((10,)), DMA((2,)),
             DMA((2, 3, 3)), DMA((2, 3, 3)), DMA((2, 4)), DMA((2, 4)),
-            DMA((3,)), DMA((3,)), DMA((HEADS_HERE, 3)), DMA((HEADS_HERE, 3)), DMA((8,)),
+            DMA((3, 2)), DMA((3, 2)), DMA((HEADS_HERE, 3)), DMA((HEADS_HERE, 3)), DMA((9,)),
         ],
         name="attention_forward",
         compiler_params=pltpu.CompilerParams(
@@ -627,9 +637,9 @@
 
 def backward_kernel(
     cubes, params, grad_mixed, grad_branch, small_grads, reduced,
-    grad_middle_in, tokens_in, normed_in, qkv_in, lse_in, mixed_in, mixed_out_in, w_qkv_in,
+    grad_middle_in, tokens_in, normed_in, qkv_in, lse_in, mixed_in, mixed_out_in, w_qkv_in, w_last_in,
     tokens_grad, small_first, small_last, w_grads, w_fc1_grad, w_fc2_grad,
-    grad_middle, tokens, normed, qkv, lse, mixed, mixed_out, w_qkv, own_reduced,
+    grad_middle, tokens, normed, qkv, lse, mixed, mixed_out, w_qkv, w_last, own_reduced,
     mixed_back, mixed_wide, outer_back, queries, keys_t, grad_q, grad_kv, packed_back,
     branch_in, input_back, pair_out, pair_in, far_out, far_in,
     held, arrived, held_last, arrived_last,
@@ -637,7 +647,7 @@
     w_src, w_in, w_z, w_z_in, w_y, w_y_in, w_all, column_sums,
     mix_send, mix_recv, br_send, br_recv, in_send, in_recv, sum_send, sum_recv, last_send, last_recv,
     ff_send, ff_recv, mate_sem, wx_send, wx_recv, wz_send, wz_recv, wy_send, wy_recv, wg_send, wg_recv,
-    load_sem,
+    load_sem, last_out, last_in, head_send, head_recv,
 ):
     here = Place()
     core, head, at = here.core, here.head, here.at
@@ -653,7 +663,7 @@
     pairs = (
         (qkv_in, qkv), (lse_in, lse), (mixed_in, mixed), (tokens_in, tokens), (w_qkv_in, w_qkv),
         (normed_in, normed), (mixed_out_in, mixed_out), (grad_middle_in, grad_middle),
-        (own_share(0), own_reduced.at[0]), (own_share(1), own_reduced.at[1]),
+        (own_share(0), own_reduced.at[0]), (own_share(1), own_reduced.at[1]), (w_last_in, w_last),
     )
     loads = [pltpu.make_async_copy(src, dst, load_sem.at[k]) for k, (src, dst) in enumerate(pairs)]
     for copy in loads:
@@ -893,26 +903,37 @@
             grad_q[chunk, 0:64] = dot_nn(keys_t[h], grad_scores).T * 0.125
 
         both = grad_kv[...]
-        packed_back[:, 0:128] = jnp.where(lane < 64, grad_q[...], both).astype(bf16)
+        first = jnp.where(lane < 64, grad_q[...], both)
+        packed_back[:, 0:128] = first.astype(bf16)
         packed_back[:, 128:192] = both[:, 0:64].astype(bf16)
-        for half in (1 - chip, chip):
-            share = dot_nn(
-                packed_back[pl.ds(pl.multiple_of(half * 784, 16), 784), :],
-                w_qkv[pl.ds(pl.multiple_of(h * 192, 16), 192), :],
-            )
-            for j in (0, 1):
-                some = share[j * ROWS : j * ROWS + ROWS]
-
-                @pl.when(h == 0)
-                def _():
-                    input_back[half, j] = some
-
-                @pl.when(h > 0)
-                def _():
-                    input_back[half, j] += some
-
-            k = 0 if half is not chip else 1
-            pl.when(h == HEADS_HERE - 1)(partial(pair_start, k, half))
+        @pl.when(h < HEADS_HERE - 1)
+        def _():
+            for k, half in enumerate((1 - chip, chip)):
+                share = dot_nn(
+                    packed_back[pl.ds(pl.multiple_of(half * 784, 16), 784), :],
+                    w_qkv[pl.ds(pl.multiple_of(h * 192, 16), 192), :],
+                )
+                for j in (0, 1):
+                    some = share[j * ROWS : j * ROWS + ROWS]
+
+                    @pl.when(h == 0)
+                    def _():
+                        input_back[half, j] = some
+
+                    @pl.when(h > 0)
+                    def _():
+                        input_back[half, j] += some
+
+                pl.when(h == HEADS_HERE - 2)(partial(pair_start, k, half))
+
+        @pl.when(h == HEADS_HERE - 1)
+        def _():
+            for j in range(4):
+                own = slice(j * ROWS, j * ROWS + ROWS)
+                last_out[j] = jnp.concatenate([first[own], both[own, 0:64]], axis=1).astype(bf16)
+            for way in (1, 2, 0):
+                head_copy(way).start()
+
         column_sums[pl.ds(h, 1), :] = jnp.sum(packed_back[...].astype(f32), axis=0, keepdims=True)
         w_grad = dot_tn(packed_back[...], normed[...])
         for n in range(HEADS_HERE):
@@ -928,6 +949,9 @@
             outer_in(2)
             sum_on(1)
             branch_on()
+            pair_copies[0].wait_recv()
+            far_out[...] = (input_back[1 - chip, core] + pair_in[0].astype(f32)).astype(bf16)
+            far_copy.start()
 
         return carry
 
@@ -936,15 +960,18 @@
     ]
     far_copy = remote(far_out, far_in, in_send.at[2], in_recv.at[2], here.along("y", 2))
 
+    def head_copy(way):
+        other, device = (
+            (mate, here.partner()), (far, here.along("y", 2)), (far_mate, here.across()),
+        )[way]
+        return remote(last_out.at[other], last_in.at[head], head_send.at[way], head_recv.at[way], device)
+
     def pair_start(k, half):
         pair_out[k] = input_back[half, 1 - core].astype(bf16)
         pair_copies[k].start()
 
     lax.fori_loop(0, HEADS_HERE, attend, 0)
 
-    pair_copies[0].wait_recv()
-    far_out[...] = (input_back[1 - chip, core] + pair_in[0].astype(f32)).astype(bf16)
-    far_copy.start()
     ff_on(0)
     branch_end()
     w_second(1)
@@ -961,9 +988,14 @@
     start = jnp.where(masked > 0.5, params[MASK : MASK + 1, 0:D], tokens[...].astype(f32))
     unit1, inverse1 = unit_of(start)
     pair_copies[1].wait_recv()
-    near = input_back[chip, core] + pair_in[1].astype(f32)
     far_copy.wait_recv()
-    back = near + far_in[...].astype(f32)
+    last_in[head] = last_out[head]
+    loads[10].wait()
+    back = input_back[chip, core] + pair_in[1].astype(f32) + far_in[...].astype(f32)
+    for way in range(3):
+        head_copy(way).wait_recv()
+    for j in range(4):
+        back = back + dot_nn(last_in[j], w_last[j])
     grad_start = grad_middle[...] + unit_back(
         back * params[GAIN1 : GAIN1 + 1, 0:D], unit1, inverse1
     )
@@ -1019,6 +1051,8 @@
     last.drain()
     for copy in [br_near, br_far, br_pass, far_copy, mate_copy] + pair_copies:
         copy.wait_send()
+    for way in range(3):
+        head_copy(way).wait_send()
     for h in range(HEADS_HERE):
         for way in range(3):
             mix_copy(h, way).wait_send()
@@ -1044,6 +1078,7 @@
         ((HEADS_HERE, TOK, 64), f32),
         ((HEADS_HERE, 4, ROWS, 64), bf16),
         ((576, D), bf16),
+        ((4, 192, D), bf16),
     )
     return pl.pallas_call(
         backward_kernel,
@@ -1055,7 +1090,7 @@
             shape((24, D), f32),
             shape((24, D), f32),
         ),
-        in_specs=[VM] * 5 + [ANY] * 9,
+        in_specs=[VM] * 5 + [ANY] * 10,
         out_specs=(VM,) * 6,
         scratch_shapes=[pltpu.VMEM(*k) for k in loaded]
         + [
@@ -1097,7 +1132,10 @@
             DMA((10,)), DMA((10,)), DMA((10,)), DMA((10,)),
             DMA((2, 3, 3)), DMA((2, 3, 3)), DMA((2,)),
             DMA((4, 3)), DMA((4, 3)), DMA((4, 3)), DMA((4, 3)), DMA((4,)), DMA((4,)), DMA((4, 3)), DMA((4, 3)),
-            DMA((10,)),
+            DMA((11,)),
+            pltpu.VMEM((4, ROWS, 192), bf16),
+            pltpu.VMEM((4, ROWS, 192), bf16),
+            DMA((3,)), DMA((3,)),
         ],
         name="attention_backward",
         compiler_params=pltpu.CompilerParams(
@@ -1170,19 +1208,19 @@
     tokens, cube_mask, mask_token, norm1_gain, norm1_bias, w_qkv, qv_bias, w_out, proj_bias,
     norm2_gain, norm2_bias, w_fc1, fc1_bias, w_fc2, fc2_bias, cotangent,
 ):
-    small = jnp.concatenate(
-        [mask_token, norm1_gain, norm1_bias, proj_bias, norm2_gain, norm2_bias, fc2_bias, fc1_bias]
-    ).astype(f32)
+    small = jnp.stack(
+        [mask_token, norm1_gain, norm1_bias, proj_bias, norm2_gain, norm2_bias, fc2_bias, fc2_bias]
+    )
     w_qkv_t = w_qkv.T
-    params, normed, qkv, lse, mixed, mixed_out, mixed_in, w_out_all, weights = forward_call(
-        small, cube_mask, tokens, w_qkv_t, qv_bias, w_out, w_fc1.T, w_fc2,
+    params, normed, qkv, lse, mixed, mixed_out, mixed_in, w_out_all, w_last_all, weights = forward_call(
+        small, fc1_bias[None], cube_mask, tokens, w_qkv_t, qv_bias, w_out, w_fc1.T, w_fc2,
     )
     block_out, grad_middle, grad_branch, grad_mixed, small_grads, reduced = feed_forward_call(
         cube_mask, params, tokens, cotangent, mixed_in, w_out_all, weights.reshape(6, 64, 96, 128),
     )
     tokens_grad, small_first, small_last, w_grads, w_fc1_grad, w_fc2_grad = backward_call(
         cube_mask, params, grad_mixed, grad_branch, small_grads, reduced.reshape(3, 4, 4, 4, 96, 128),
-        grad_middle, tokens, normed.reshape(TOK, D), qkv, lse, mixed, mixed_out, w_qkv_t,
+        grad_middle, tokens, normed.reshape(TOK, D), qkv, lse, mixed, mixed_out, w_qkv_t, w_last_all,
     )
     outs = list(
         results_call(block_out, tokens_grad, w_grads, w_fc1_grad, w_fc2_grad, small_first, small_last)

time: 190 us -> 176 us (0.926)
  Pallas kernels: 182 us -> 174 us
  local copies, waits for them, and re-layouts: 5.43 us -> 1.37 us
    pallas_call x1, Pallas kernels: 88.5 us -> 80 us  [backward_call(): pl.pallas_call(backward_kernel, out_shape=(shape((ROWS, D), f32), shape((...]
    concatenate x1 -> x0, local copies, waits for them, and re-layouts: 5.43 us -> none  [body(): jnp.concatenate([mask_token, norm1_gain, norm1_bias, proj_bias, norm2_gai...]
where the time goes in v3:
time: 176 us
  Pallas kernels  174 us (99%)
    pallas_call x1, Pallas kernels, backward_call(): pl.pallas_call(backward_kernel, out_shape=(shape((ROWS, D), f32), shape((...  80 us
    pallas_call x1, Pallas kernels, forward_call(): pl.pallas_call(forward_kernel, out_shape=(shape((8, D + UNITS), f32),) +...  64.7 us
    pallas_call x1, Pallas kernels, feed_forward_call(): pl.pallas_call(feed_forward_kernel, out_shape=(shape((ROWS, D), f32), sha...  24.8 us
    pallas_call x1, Pallas kernels, results_call(): pl.pallas_call(results_kernel, out_shape=(shape((ROWS, D), f32), shape((R...  4.56 us

profile of v3, /device:TPU:0, one launch (start us, length us, event | category | flops | bytes accessed | tf_op | source)
XLA Modules:
  0.0 176.3 jit_solution(2150552240369873119)
XLA Ops:
  0.6 1.4 stack.32.small
  2.0 64.7 %attention_forward.1 = (f32[8,1152]{1,0:T(8,128)}, bf16[2,784,768]{2,1,0:T(8,128)(2,1)}, bf16[9,1568,64]{2,1,0:T(8,128)(2,1)}, f32[21,8,224]{2,1,0:T(8,128)}, f3...) custom-call(bf16[8,6]{1,0:T(8,128)(2,1)} %stack.32.small, ...), custom_call_target="tpu_custom_call" | custom-call | tf_op jit(solution)/shard_map/attention_forward/pallas_call | solution.py:449
  66.7 24.8 %feed_forward.1 = (f32[392,768]{1,0:T(8,128)}, f32[392,768]{1,0:T(8,128)}, bf16[392,768]{1,0:T(8,128)(2,1)}, bf16[3,4,392,64]{3,2,1,0:T(8,128)(2,1)}, f32[8,1152...) custom-call(s32[1,196]{1,0:T(1,128)} %cubes.5, f32[8,1152]{1,0:T(8,128)} %get-tuple-element.52.params, ...), custom_call_target="tpu_custom_call" | custom-call | tf_op jit(solution)/shard_map/feed_forward/pallas_call | solution.py:605
  91.5 80.0 %attention_backward.1 = (f32[392,768]{1,0:T(8,128)}, f32[8,1152]{1,0:T(8,128)}, f32[8,640]{1,0:T(8,128)}, bf16[4,4,288,128]{3,2,1,0:T(8,128)(2,1)}, f32[24,768]{1,0:T(8,128)}, /*index=5*/f32[24,768]{1,0:T(8,128)}) custom-call(s32[1,196]{1,0:T(1,128)} %cubes.5, f32[8,1152]{1,0:T(8,128)} %get-tuple-element.52.params, ...), custom_call_target="tpu_custom_call" | custom-call | tf_op jit(solution)/shard_map/attention_backward/pallas_call | solution.py:1083
  171.5 4.6 %results.1 = (f32[392,768]{1,0:T(8,128)}, f32[392,768]{1,0:T(8,128)}, f32[1,6]{1,0:T(1,128)}, f32[1,6]{1,0:T(1,128)}, f32[1,6]{1,0:T(1,128)}, /*index=5*/f32[576...) custom-call(f32[392,768]{1,0:T(8,128)} %get-tuple-element.56.block_i, ...), custom_call_target="tpu_custom_call" | custom-call | tf_op jit(solution)/shard_map/results/pallas_call | solution.py:1193

commit v4 on v3

--- a/solution.py
+++ b/solution.py
@@ -163,12 +163,12 @@
 
 def forward_kernel(
     small, fc1_bias, cubes, tokens, w_qkv, qv_bias, w_out, w_fc1, w_fc2,
-    params, normed_out, qkv_out, lse_out, mixed_keep, mixed_out_keep, mixed_in_out, w_out_all_out,
+    params, normed_out, qkv_out, lse_out, mixed_keep, pair_keep, last_keep, pair_in_out, last_in_out, w_out_all_out,
     w_last_all_out, gathered,
-    normed, qkv, lse, mixed, mixed_out, mixed_in, w_out_all, w_last_all,
+    normed, qkv, lse, mixed, pair_out, last_out, pair_in, last_in, w_out_all, w_last_all,
     rows, held, arrived, own_half, their_half, chip_block, block, values_t,
     tok_send, tok_recv, sum_send, sum_recv, half_sem, ff_send, ff_recv, fwd_send, fwd_recv,
-    out_send, out_recv, mix_send, mix_recv, local_sem,
+    out_send, out_recv, mix_send, mix_recv, local_sem, on_send, on_recv,
 ):
     here = Place()
     core, head = here.core, here.head
@@ -245,8 +245,18 @@
         spot = gathered.at[(ours,) + plane + (of_kind,)]
         return remote(spot, spot, fwd_send.at[kind, step], fwd_recv.at[kind, step], here.partner())
 
+    def onward_copy(kind, way):
+        last = GATHER[kind][2]
+        from_slot = slot_of(last, (at[last] + (3 if way == 0 else 1)) % 4)
+        plane = region({last: from_slot, "y": pl.ds(2 * way, 2)})
+        spot = gathered.at[(ours,) + plane + (pl.ds(kind * 48, 48),)]
+        return remote(
+            spot, spot, on_send.at[kind, way], on_recv.at[kind, way],
+            here.along(last, 1 if way == 0 else 3),
+        )
+
     def ff_start(phase):
-        for step in (1, 2, 3):
+        for step in (1, 3) if phase == 2 else (1, 3, 2):
             for kind in (0, 1):
                 ff_copy(kind, phase, step).start()
 
@@ -338,25 +348,35 @@
     for h in range(HEADS_HERE):
         values_t[h] = jnp.concatenate([qkv[h * 3 + 2].astype(f32).T, ones_row], axis=0).astype(bf16)
 
-    def mix_copy(h, way):
+    def mix_copy(k, way):
         other, device = (
             (mate, here.partner()), (far, here.along("y", 2)), (far_mate, here.across()),
         )[way]
-        return remote(
-            mixed_out.at[h, other], mixed_in.at[h, head], mix_send.at[h, way], mix_recv.at[h, way], device
-        )
-
-    def mix_start(h):
+        src, dst = ((pair_out, pair_in), (last_out, last_in))[k]
+        return remote(src.at[other], dst.at[head], mix_send.at[k, way], mix_recv.at[k, way], device)
+
+    def mix_start(k):
         for j in range(4):
-            mixed_out[h, j] = mixed[h, j * ROWS : j * ROWS + ROWS, :].astype(bf16)
+            own = slice(j * ROWS, j * ROWS + ROWS)
+            if k == 0:
+                pair_out[j] = jnp.concatenate([mixed[0, own, :], mixed[1, own, :]], axis=1).astype(bf16)
+            else:
+                last_out[j] = mixed[2, own, :].astype(bf16)
         for way in (1, 2, 0):
-            mix_copy(h, way).start()
-        mixed_in[h, head] = mixed_out[h, head]
-
-    def ff_pass(step):
-        for kind in (0, 1):
-            ff_copy(kind, 2, step).wait_recv()
-            pass_copy(kind, step).start()
+            mix_copy(k, way).start()
+        if k == 0:
+            pair_in[head] = pair_out[head]
+        else:
+            last_in[head] = last_out[head]
+
+    def ff_onward():
+        for way, step in enumerate((1, 3)):
+            for kind in (0, 1):
+                ff_copy(kind, 2, step).wait_recv()
+                onward_copy(kind, way).start()
+        for step in (1, 3):
+            for kind in (0, 1):
+                pass_copy(kind, step).start()
 
     def out_on():
         for k in (0, 1):
@@ -378,23 +398,30 @@
             total = outcome[64:65, :]
             mixed[h, k * QCHUNK : k * QCHUNK + QCHUNK, :] = (outcome[0:64, :] / total).T
             lse[h * CHUNKS + k] = jnp.broadcast_to(top + jnp.log(total), (8, QCHUNK))
-        for n in range(HEADS_HERE - 1):
-            pl.when(h == n)(partial(mix_start, n))
-        pl.when(h == 1)(out_on)
+        pl.when(h == 0)(ff_onward)
+
+        @pl.when(h == 1)
+        def _():
+            mix_start(0)
+            out_on()
+
         return carry
 
     lax.fori_loop(0, HEADS_HERE, attend, 0)
 
-    mix_start(HEADS_HERE - 1)
-    for step in (1, 2, 3):
-        ff_pass(step)
+    mix_start(1)
+    for kind in (0, 1):
+        for way in (0, 1):
+            onward_copy(kind, way).wait_recv()
+        pass_copy(kind, 2).start()
     for k in (0, 1):
         out_copy(0, k).wait_recv()
         out_copy(2, k).wait_recv()
     late = [
         pltpu.make_async_copy(lse, lse_out, local_sem.at[3]),
         pltpu.make_async_copy(mixed, mixed_keep, local_sem.at[4]),
-        pltpu.make_async_copy(mixed_out, mixed_out_keep, local_sem.at[5]),
+        pltpu.make_async_copy(pair_out, pair_keep, local_sem.at[5]),
+        pltpu.make_async_copy(last_out, last_keep, local_sem.at[9]),
         pltpu.make_async_copy(w_out_all, w_out_all_out, local_sem.at[6]),
         pltpu.make_async_copy(w_last_all, w_last_all_out, local_sem.at[8]),
     ]
@@ -403,26 +430,32 @@
     for kind in (0, 1):
         for step in range(4):
             pass_copy(kind, step).wait_recv()
-    for h in range(HEADS_HERE):
+    for k in (0, 1):
         for way in range(3):
-            mix_copy(h, way).wait_recv()
-    last_copy = pltpu.make_async_copy(mixed_in, mixed_in_out, local_sem.at[7])
-    last_copy.start()
+            mix_copy(k, way).wait_recv()
+    last_copies = [
+        pltpu.make_async_copy(pair_in, pair_in_out, local_sem.at[7]),
+        pltpu.make_async_copy(last_in, last_in_out, local_sem.at[10]),
+    ]
+    for copy in last_copies:
+        copy.start()
     sums.drain()
     half_copy.wait_send()
     for way in range(3):
         for k in (0, 1):
             out_copy(way, k).wait_send()
             tok_copy(way, k).wait_send()
-        for h in range(HEADS_HERE):
-            mix_copy(h, way).wait_send()
+        for k in (0, 1):
+            mix_copy(k, way).wait_send()
     for kind in (0, 1):
         for phase in range(3):
-            for step in (1, 2, 3):
+            for step in (1, 3) if phase == 2 else (1, 2, 3):
                 ff_copy(kind, phase, step).wait_send()
+        for way in (0, 1):
+            onward_copy(kind, way).wait_send()
         for step in range(4):
             pass_copy(kind, step).wait_send()
-    for copy in early + late + [last_copy]:
+    for copy in early + late + last_copies:
         copy.wait()
 
 
@@ -441,8 +474,10 @@
         ((9, TOK, 64), bf16),
         ((HEADS_HERE * CHUNKS, 8, QCHUNK), f32),
         ((HEADS_HERE, TOK, 64), f32),
-        ((HEADS_HERE, 4, ROWS, 64), bf16),
-        ((HEADS_HERE, 4, ROWS, 64), bf16),
+        ((4, ROWS, 128), bf16),
+        ((4, ROWS, 64), bf16),
+        ((4, ROWS, 128), bf16),
+        ((4, ROWS, 64), bf16),
         ((4, 192, D), bf16),
         ((4, 192, D), bf16),
     )
@@ -452,7 +487,7 @@
         + tuple(shape(*k) for k in kept)
         + (shape((6, 4, 4, 4, 96, 128)),),
         in_specs=[VM] * 9,
-        out_specs=(VM,) + (ANY,) * 9,
+        out_specs=(VM,) + (ANY,) * 11,
         scratch_shapes=[pltpu.VMEM(*k) for k in kept]
         + [
             pltpu.VMEM((4, ROWS, D), bf16),
@@ -465,7 +500,7 @@
             pltpu.VMEM((HEADS_HERE, 80, TOK), bf16),
             DMA((3, 2)), DMA((3, 2)), DMA((10,)), DMA((10,)), DMA((2,)),
             DMA((2, 3, 3)), DMA((2, 3, 3)), DMA((2, 4)), DMA((2, 4)),
-            DMA((3, 2)), DMA((3, 2)), DMA((HEADS_HERE, 3)), DMA((HEADS_HERE, 3)), DMA((9,)),
+            DMA((3, 2)), DMA((3, 2)), DMA((2, 3)), DMA((2, 3)), DMA((11,)), DMA((2, 2)), DMA((2, 2)),
         ],
         name="attention_forward",
         compiler_params=pltpu.CompilerParams(
@@ -479,8 +514,8 @@
 
 
 def feed_forward_kernel(
-    cubes, params, tokens, cotangent, mixed_in, w_out_all, weights,
-    block_out, grad_middle, grad_branch, grad_mixed, small_grads, reduced_out,
+    cubes, params, tokens, cotangent, pair_in, last_in, w_out_all, weights,
+    block_out, grad_middle, grad_branch, grad_pair, grad_last, small_grads, reduced_out,
     held, grads, arrived, reduced, normed2, outer, grad_normed2,
     load_sem, pair_send, pair_recv, keep_sem,
 ):
@@ -500,7 +535,7 @@
     start = jnp.where(masked > 0.5, params[MASK : MASK + 1, 0:D], tokens[...].astype(f32))
     branch = jnp.zeros((ROWS, D), f32)
     for j in range(4):
-        some = jnp.concatenate([mixed_in[h, j] for h in range(HEADS_HERE)], axis=1)
+        some = jnp.concatenate([pair_in[j], last_in[j]], axis=1)
         branch = branch + dot_nn(some, w_out_all[j])
     middle = start + branch + params[PROJ : PROJ + 1, 0:D]
     gain2 = params[GAIN2 : GAIN2 + 1, 0:D]
@@ -588,8 +623,8 @@
     grad_branch[...] = low
     for j in range(4):
         some = dot_nt(low, w_out_all[j]).astype(bf16)
-        for h in range(HEADS_HERE):
-            grad_mixed[h, j] = some[:, h * 64 : h * 64 + 64]
+        grad_pair[j] = some[:, 0:128]
+        grad_last[j] = some[:, 128:192]
     sums = [
         jnp.sum(v, axis=0, keepdims=True)
         for v in (grad_mid, back * unit2, back, grad_out)
@@ -608,12 +643,13 @@
             shape((ROWS, D), f32),
             shape((ROWS, D), f32),
             shape((ROWS, D)),
-            shape((HEADS_HERE, 4, ROWS, 64)),
+            shape((4, ROWS, 128)),
+            shape((4, ROWS, 64)),
             shape((8, D + UNITS), f32),
             shape((3, 64, 96, 128)),
         ),
-        in_specs=[VM] * 6 + [ANY],
-        out_specs=(VM,) * 5 + (ANY,),
+        in_specs=[VM] * 7 + [ANY],
+        out_specs=(VM,) * 6 + (ANY,),
         scratch_shapes=[
             pltpu.VMEM((6, 64, 96, 128), bf16),
             pltpu.VMEM((6, 64, 96, 128), bf16),
@@ -636,11 +672,11 @@
 
 
 def backward_kernel(
-    cubes, params, grad_mixed, grad_branch, small_grads, reduced,
-    grad_middle_in, tokens_in, normed_in, qkv_in, lse_in, mixed_in, mixed_out_in, w_qkv_in, w_last_in,
+    cubes, params, grad_pair, grad_last, grad_branch, small_grads, reduced,
+    grad_middle_in, tokens_in, normed_in, qkv_in, lse_in, mixed_in, pair_in_, last_in_, w_qkv_in, w_last_in,
     tokens_grad, small_first, small_last, w_grads, w_fc1_grad, w_fc2_grad,
-    grad_middle, tokens, normed, qkv, lse, mixed, mixed_out, w_qkv, w_last, own_reduced,
-    mixed_back, mixed_wide, outer_back, queries, keys_t, grad_q, grad_kv, packed_back,
+    grad_middle, tokens, normed, qkv, lse, mixed, mixed_pair, mixed_last, w_qkv, w_last, own_reduced,
+    pair_back, last_back, mixed_wide, outer_back, queries, keys_t, grad_q, grad_kv, packed_back,
     branch_in, input_back, pair_out, pair_in, far_out, far_in,
     held, arrived, held_last, arrived_last,
     ff_in0, ff_sum1, ff_in1, ff_sum2, ff_in2, ff_last, ff_mate,
@@ -662,25 +698,25 @@
 
     pairs = (
         (qkv_in, qkv), (lse_in, lse), (mixed_in, mixed), (tokens_in, tokens), (w_qkv_in, w_qkv),
-        (normed_in, normed), (mixed_out_in, mixed_out), (grad_middle_in, grad_middle),
+        (normed_in, normed), (pair_in_, mixed_pair), (grad_middle_in, grad_middle),
         (own_share(0), own_reduced.at[0]), (own_share(1), own_reduced.at[1]), (w_last_in, w_last),
+        (last_in_, mixed_last),
     )
     loads = [pltpu.make_async_copy(src, dst, load_sem.at[k]) for k, (src, dst) in enumerate(pairs)]
     for copy in loads:
         copy.start()
     greet(here)
 
-    def mix_copy(h, way):
+    def mix_copy(k, way):
         other, device = (
             (mate, here.partner()), (far, here.along("y", 2)), (far_mate, here.across()),
         )[way]
-        return remote(
-            grad_mixed.at[h, other], mixed_back.at[h, head], mix_send.at[h, way], mix_recv.at[h, way], device
-        )
-
-    for h in range(HEADS_HERE):
+        src, dst = ((grad_pair, pair_back), (grad_last, last_back))[k]
+        return remote(src.at[other], dst.at[head], mix_send.at[k, way], mix_recv.at[k, way], device)
+
+    for k in (0, 1):
         for way in (1, 2, 0):
-            mix_copy(h, way).start()
+            mix_copy(k, way).start()
 
     def peer_slot(axis, step):
         return slot_of(axis, (at[axis] + step) % 4)
@@ -825,8 +861,8 @@
     br_far = remote(grad_branch, branch_in.at[head], br_send.at[1], br_recv.at[1], here.along("y", 2))
     br_pass = remote(branch_in.at[far], branch_in.at[far], br_send.at[2], br_recv.at[2], here.partner())
     branch_in[head] = grad_branch[...]
-    for h in range(HEADS_HERE):
-        mixed_back[h, head] = grad_mixed[h, head]
+    pair_back[head] = grad_pair[head]
+    last_back[head] = grad_last[head]
 
     zeros = jnp.zeros((TOK, 64), bf16)
     loads[0].wait()
@@ -836,16 +872,19 @@
         keys_t[h] = qkv[h * 3 + 1].astype(f32).T.astype(bf16)
 
     def outer_in(h):
-        for way in range(3):
-            mix_copy(h, way).wait_recv()
+        if h != 1:
+            for way in range(3):
+                mix_copy(h // 2, way).wait_recv()
         for j in range(4):
-            mixed_wide[j * ROWS : j * ROWS + ROWS, :] = mixed_back[h, j].astype(f32)
+            block = last_back[j] if h == 2 else pair_back[j]
+            lanes = slice(64, 128) if h == 1 else slice(0, 64)
+            mixed_wide[j * ROWS : j * ROWS + ROWS, :] = block.astype(f32)[:, lanes]
         outer_back[h] = jnp.concatenate([mixed_wide[...].astype(bf16), zeros], axis=1)
 
     outer_in(0)
     br_far.start()
     br_near.start()
-    for k in (1, 2, 3, 4, 5, 6, 7):
+    for k in (1, 2, 3, 4, 5, 6, 7, 11):
         loads[k].wait()
 
     def branch_on():
@@ -857,7 +896,7 @@
         br_pass.wait_recv()
         grad = jnp.zeros((192, D), f32)
         for j in range(4):
-            some = jnp.concatenate([mixed_out[h, j] for h in range(HEADS_HERE)], axis=1)
+            some = jnp.concatenate([mixed_pair[j], mixed_last[j]], axis=1)
             grad = grad + dot_tn(some, branch_in[j])
         w_begin(0, grad)
 
@@ -972,17 +1011,16 @@
 
     lax.fori_loop(0, HEADS_HERE, attend, 0)
 
-    ff_on(0)
     branch_end()
     w_second(1)
     w_second(2)
+    ff_on(0)
     sum_on(2)
-    ff_on(1)
     w_second(3)
     w_third(1)
     w_third(2)
+    w_second(0)
     sum_on(3)
-    w_second(0)
 
     masked = row_mask(cubes, head)
     start = jnp.where(masked > 0.5, params[MASK : MASK + 1, 0:D], tokens[...].astype(f32))
@@ -1020,32 +1058,33 @@
     w_third(3)
     last.finish(0)
     last.start(1)
+    w_third(0)
     w_fourth(1)
     w_fourth(2)
+    ff_on(1)
+    last.finish(1)
+    last.start(2)
+    w_fourth(3)
+    w_fourth(0)
     ff_on(2)
     mate_copy = remote(
         ff_last.at[:, pl.ds(pl.multiple_of((1 - core) * 24, 8), 24), :], ff_mate,
         mate_sem.at[0], mate_sem.at[1], here.partner(),
     )
     mate_copy.start()
-    last.finish(1)
-    last.start(2)
-    w_third(0)
-    w_fourth(3)
     last.finish(2)
     last.start(3)
-    w_fourth(0)
+    w_end(1)
+    w_end(2)
+    w_end(3)
     mate_copy.wait_recv()
     for kind, target in ((0, w_fc1_grad), (1, w_fc2_grad)):
         target[:, pl.ds(pl.multiple_of(core * UNITS, UNITS), UNITS)] = ff_last[
             kind, pl.ds(pl.multiple_of(core * 24, 8), 24), :
         ]
         target[:, pl.ds(pl.multiple_of((1 - core) * UNITS, UNITS), UNITS)] = ff_mate[kind]
-    w_end(1)
-    w_end(2)
+    w_end(0)
     small_last[...] = last.finish(3)
-    w_end(3)
-    w_end(0)
 
     sums.drain()
     last.drain()
@@ -1053,9 +1092,9 @@
         copy.wait_send()
     for way in range(3):
         head_copy(way).wait_send()
-    for h in range(HEADS_HERE):
+    for k in (0, 1):
         for way in range(3):
-            mix_copy(h, way).wait_send()
+            mix_copy(k, way).wait_send()
     for kind in (0, 1):
         for phase in range(3):
             for step in (1, 2, 3):
@@ -1076,7 +1115,8 @@
         ((9, TOK, 64), bf16),
         ((HEADS_HERE * CHUNKS, 8, QCHUNK), f32),
         ((HEADS_HERE, TOK, 64), f32),
-        ((HEADS_HERE, 4, ROWS, 64), bf16),
+        ((4, ROWS, 128), bf16),
+        ((4, ROWS, 64), bf16),
         ((576, D), bf16),
         ((4, 192, D), bf16),
     )
@@ -1090,12 +1130,13 @@
             shape((24, D), f32),
             shape((24, D), f32),
         ),
-        in_specs=[VM] * 5 + [ANY] * 10,
+        in_specs=[VM] * 6 + [ANY] * 11,
         out_specs=(VM,) * 6,
         scratch_shapes=[pltpu.VMEM(*k) for k in loaded]
         + [
             pltpu.VMEM((2, 3, 4, 4, 48, 128), bf16),
-            pltpu.VMEM((HEADS_HERE, 4, ROWS, 64), bf16),
+            pltpu.VMEM((4, ROWS, 128), bf16),
+            pltpu.VMEM((4, ROWS, 64), bf16),
             pltpu.VMEM((TOK, 64), f32),
             pltpu.VMEM((HEADS_HERE, TOK, 128), bf16),
             pltpu.VMEM((HEADS_HERE, TOK, 128), bf16),
@@ -1128,11 +1169,11 @@
             pltpu.VMEM((4, 288, 128), bf16),
             pltpu.VMEM((4, 4, 288, 128), bf16),
             pltpu.VMEM((8, 192), f32),
-            DMA((HEADS_HERE, 3)), DMA((HEADS_HERE, 3)), DMA((3,)), DMA((3,)), DMA((3,)), DMA((3,)),
+            DMA((2, 3)), DMA((2, 3)), DMA((3,)), DMA((3,)), DMA((3,)), DMA((3,)),
             DMA((10,)), DMA((10,)), DMA((10,)), DMA((10,)),
             DMA((2, 3, 3)), DMA((2, 3, 3)), DMA((2,)),
             DMA((4, 3)), DMA((4, 3)), DMA((4, 3)), DMA((4, 3)), DMA((4,)), DMA((4,)), DMA((4, 3)), DMA((4, 3)),
-            DMA((11,)),
+            DMA((12,)),
             pltpu.VMEM((4, ROWS, 192), bf16),
             pltpu.VMEM((4, ROWS, 192), bf16),
             DMA((3,)), DMA((3,)),
@@ -1212,15 +1253,18 @@
         [mask_token, norm1_gain, norm1_bias, proj_bias, norm2_gain, norm2_bias, fc2_bias, fc2_bias]
     )
     w_qkv_t = w_qkv.T
-    params, normed, qkv, lse, mixed, mixed_out, mixed_in, w_out_all, w_last_all, weights = forward_call(
+    (
+        params, normed, qkv, lse, mixed, pair_out, last_out, pair_in, last_in, w_out_all, w_last_all, weights,
+    ) = forward_call(
         small, fc1_bias[None], cube_mask, tokens, w_qkv_t, qv_bias, w_out, w_fc1.T, w_fc2,
     )
-    block_out, grad_middle, grad_branch, grad_mixed, small_grads, reduced = feed_forward_call(
-        cube_mask, params, tokens, cotangent, mixed_in, w_out_all, weights.reshape(6, 64, 96, 128),
+    block_out, grad_middle, grad_branch, grad_pair, grad_last, small_grads, reduced = feed_forward_call(
+        cube_mask, params, tokens, cotangent, pair_in, last_in, w_out_all, weights.reshape(6, 64, 96, 128),
     )
     tokens_grad, small_first, small_last, w_grads, w_fc1_grad, w_fc2_grad = backward_call(
-        cube_mask, params, grad_mixed, grad_branch, small_grads, reduced.reshape(3, 4, 4, 4, 96, 128),
-        grad_middle, tokens, normed.reshape(TOK, D), qkv, lse, mixed, mixed_out, w_qkv_t, w_last_all,
+        cube_mask, params, grad_pair, grad_last, grad_branch, small_grads, reduced.reshape(3, 4, 4, 4, 96, 128),
+        grad_middle, tokens, normed.reshape(TOK, D), qkv, lse, mixed, pair_out, last_out,
+        w_qkv_t, w_last_all,
     )
     outs = list(
         results_call(block_out, tokens_grad, w_grads, w_fc1_grad, w_fc2_grad, small_first, small_last)

time: 176 us -> 173 us (0.983)
  Pallas kernels: 174 us -> 171 us
where the time goes in v4:
time: 173 us
  Pallas kernels  171 us (99%)
    pallas_call x1, Pallas kernels, backward_call(): pl.pallas_call(backward_kernel, out_shape=(shape((ROWS, D), f32), shape((...  79.1 us
    pallas_call x1, Pallas kernels, forward_call(): pl.pallas_call(forward_kernel, out_shape=(shape((8, D + UNITS), f32),) +...  64.3 us
    pallas_call x1, Pallas kernels, feed_forward_call(): pl.pallas_call(feed_forward_kernel, out_shape=(shape((ROWS, D), f32), sha...  23 us
    pallas_call x1, Pallas kernels, results_call(): pl.pallas_call(results_kernel, out_shape=(shape((ROWS, D), f32), shape((R...  4.56 us

profile of v4, /device:TPU:0, one launch (start us, length us, event | category | flops | bytes accessed | tf_op | source)
XLA Modules:
  0.0 173.2 jit_solution(3165139139210691717)
XLA Ops:
  0.6 1.4 stack.32.small
  2.0 64.3 %attention_forward.1 = (f32[8,1152]{1,0:T(8,128)}, bf16[2,784,768]{2,1,0:T(8,128)(2,1)}, bf16[9,1568,64]{2,1,0:T(8,128)(2,1)}, f32[21,8,224]{2,1,0:T(8,128)}, f3...) custom-call(bf16[8,6]{1,0:T(8,128)(2,1)} %stack.32.small, ...), custom_call_target="tpu_custom_call" | custom-call | tf_op jit(solution)/shard_map/attention_forward/pallas_call | solution.py:484
  66.3 23.0 %feed_forward.1 = (f32[392,768]{1,0:T(8,128)}, f32[392,768]{1,0:T(8,128)}, bf16[392,768]{1,0:T(8,128)(2,1)}, bf16[4,392,128]{2,1,0:T(8,128)(2,1)}, bf16[4,392,64...) custom-call(s32[1,196]{1,0:T(1,128)} %cubes.5, f32[8,1152]{1,0:T(8,128)} %get-tuple-element.55.params, ...), custom_call_target="tpu_custom_call" | custom-call | tf_op jit(solution)/shard_map/feed_forward/pallas_call | solution.py:640
  89.4 79.1 %attention_backward.1 = (f32[392,768]{1,0:T(8,128)}, f32[8,1152]{1,0:T(8,128)}, f32[8,640]{1,0:T(8,128)}, bf16[4,4,288,128]{3,2,1,0:T(8,128)(2,1)}, f32[24,768]{1,0:T(8,128)}, /*index=5*/f32[24,768]{1,0:T(8,128)}) custom-call(s32[1,196]{1,0:T(1,128)} %cubes.5, f32[8,1152]{1,0:T(8,128)} %get-tuple-element.55.params, ...), custom_call_target="tpu_custom_call" | custom-call | tf_op jit(solution)/shard_map/attention_backward/pallas_call | solution.py:1123
  168.5 4.6 %results.1 = (f32[392,768]{1,0:T(8,128)}, f32[392,768]{1,0:T(8,128)}, f32[1,6]{1,0:T(1,128)}, f32[1,6]{1,0:T(1,128)}, f32[1,6]{1,0:T(1,128)}, /*index=5*/f32[576...) custom-call(f32[392,768]{1,0:T(8,128)} %get-tuple-element.60.block_i, ...), custom_call_target="tpu_custom_call" | custom-call | tf_op jit(solution)/shard_map/results/pallas_call | solution.py:1234

commit v5 on v4

--- a/solution.py
+++ b/solution.py
@@ -38,6 +38,17 @@
 
 def dot_tn(left, right):
     return lax.dot_general(left, right, (((0,), (0,)), ((), ())), preferred_element_type=f32)
+
+
+def fold(values, start):
+    return jnp.concatenate(
+        [values[start : start + 200, 0:64], values[start + 192 : start + ROWS, 0:64]], axis=1
+    ).astype(bf16)
+
+
+def unfold(folded):
+    wide = folded.astype(f32)
+    return jnp.concatenate([wide[:, 0:64], wide[8:200, 64:128]], axis=0).astype(bf16)
 
 
 class Place:
@@ -361,7 +372,7 @@
             if k == 0:
                 pair_out[j] = jnp.concatenate([mixed[0, own, :], mixed[1, own, :]], axis=1).astype(bf16)
             else:
-                last_out[j] = mixed[2, own, :].astype(bf16)
+                last_out[j] = fold(mixed.at[2], j * ROWS)
         for way in (1, 2, 0):
             mix_copy(k, way).start()
         if k == 0:
@@ -475,9 +486,9 @@
         ((HEADS_HERE * CHUNKS, 8, QCHUNK), f32),
         ((HEADS_HERE, TOK, 64), f32),
         ((4, ROWS, 128), bf16),
-        ((4, ROWS, 64), bf16),
+        ((4, 200, 128), bf16),
         ((4, ROWS, 128), bf16),
-        ((4, ROWS, 64), bf16),
+        ((4, 200, 128), bf16),
         ((4, 192, D), bf16),
         ((4, 192, D), bf16),
     )
@@ -535,7 +546,7 @@
     start = jnp.where(masked > 0.5, params[MASK : MASK + 1, 0:D], tokens[...].astype(f32))
     branch = jnp.zeros((ROWS, D), f32)
     for j in range(4):
-        some = jnp.concatenate([pair_in[j], last_in[j]], axis=1)
+        some = jnp.concatenate([pair_in[j], unfold(last_in[j])], axis=1)
         branch = branch + dot_nn(some, w_out_all[j])
     middle = start + branch + params[PROJ : PROJ + 1, 0:D]
     gain2 = params[GAIN2 : GAIN2 + 1, 0:D]
@@ -683,7 +694,7 @@
     w_src, w_in, w_z, w_z_in, w_y, w_y_in, w_all, column_sums,
     mix_send, mix_recv, br_send, br_recv, in_send, in_recv, sum_send, sum_recv, last_send, last_recv,
     ff_send, ff_recv, mate_sem, wx_send, wx_recv, wz_send, wz_recv, wy_send, wy_recv, wg_send, wg_recv,
-    load_sem, last_out, last_in, head_send, head_recv,
+    load_sem, last_out, last_in, value_out, value_in, head_send, head_recv,
 ):
     here = Place()
     core, head, at = here.core, here.head, here.at
@@ -896,7 +907,7 @@
         br_pass.wait_recv()
         grad = jnp.zeros((192, D), f32)
         for j in range(4):
-            some = jnp.concatenate([mixed_pair[j], mixed_last[j]], axis=1)
+            some = jnp.concatenate([mixed_pair[j], unfold(mixed_last[j])], axis=1)
             grad = grad + dot_tn(some, branch_in[j])
         w_begin(0, grad)
 
@@ -969,11 +980,20 @@
         def _():
             for j in range(4):
                 own = slice(j * ROWS, j * ROWS + ROWS)
-                last_out[j] = jnp.concatenate([first[own], both[own, 0:64]], axis=1).astype(bf16)
+                last_out[j] = first[own].astype(bf16)
+                value_out[j] = fold(both, j * ROWS)
             for way in (1, 2, 0):
-                head_copy(way).start()
+                for k in (0, 1):
+                    head_copy(k, way).start()
 
         column_sums[pl.ds(h, 1), :] = jnp.sum(packed_back[...].astype(f32), axis=0, keepdims=True)
+
+        @pl.when(h == HEADS_HERE - 2)
+        def _():
+            pair_copies[0].wait_recv()
+            far_out[...] = (input_back[1 - chip, core] + pair_in[0].astype(f32)).astype(bf16)
+            far_copy.start()
+
         w_grad = dot_tn(packed_back[...], normed[...])
         for n in range(HEADS_HERE):
             pl.when(h == n)(partial(w_begin, n + 1, w_grad))
@@ -988,9 +1008,6 @@
             outer_in(2)
             sum_on(1)
             branch_on()
-            pair_copies[0].wait_recv()
-            far_out[...] = (input_back[1 - chip, core] + pair_in[0].astype(f32)).astype(bf16)
-            far_copy.start()
 
         return carry
 
@@ -999,11 +1016,12 @@
     ]
     far_copy = remote(far_out, far_in, in_send.at[2], in_recv.at[2], here.along("y", 2))
 
-    def head_copy(way):
+    def head_copy(k, way):
         other, device = (
             (mate, here.partner()), (far, here.along("y", 2)), (far_mate, here.across()),
         )[way]
-        return remote(last_out.at[other], last_in.at[head], head_send.at[way], head_recv.at[way], device)
+        src, dst = ((last_out, last_in), (value_out, value_in))[k]
+        return remote(src.at[other], dst.at[head], head_send.at[k, way], head_recv.at[k, way], device)
 
     def pair_start(k, half):
         pair_out[k] = input_back[half, 1 - core].astype(bf16)
@@ -1028,12 +1046,15 @@
     pair_copies[1].wait_recv()
     far_copy.wait_recv()
     last_in[head] = last_out[head]
+    value_in[head] = value_out[head]
     loads[10].wait()
     back = input_back[chip, core] + pair_in[1].astype(f32) + far_in[...].astype(f32)
     for way in range(3):
-        head_copy(way).wait_recv()
+        for k in (0, 1):
+            head_copy(k, way).wait_recv()
     for j in range(4):
-        back = back + dot_nn(last_in[j], w_last[j])
+        some = jnp.concatenate([last_in[j], unfold(value_in[j])], axis=1)
+        back = back + dot_nn(some, w_last[j])
     grad_start = grad_middle[...] + unit_back(
         back * params[GAIN1 : GAIN1 + 1, 0:D], unit1, inverse1
     )
@@ -1091,7 +1112,8 @@
     for copy in [br_near, br_far, br_pass, far_copy, mate_copy] + pair_copies:
         copy.wait_send()
     for way in range(3):
-        head_copy(way).wait_send()
+        for k in (0, 1):
+            head_copy(k, way).wait_send()
     for k in (0, 1):
         for way in range(3):
             mix_copy(k, way).wait_send()
@@ -1116,7 +1138,7 @@
         ((HEADS_HERE * CHUNKS, 8, QCHUNK), f32),
         ((HEADS_HERE, TOK, 64), f32),
         ((4, ROWS, 128), bf16),
-        ((4, ROWS, 64), bf16),
+        ((4, 200, 128), bf16),
         ((576, D), bf16),
         ((4, 192, D), bf16),
     )
@@ -1174,9 +1196,11 @@
             DMA((2, 3, 3)), DMA((2, 3, 3)), DMA((2,)),
             DMA((4, 3)), DMA((4, 3)), DMA((4, 3)), DMA((4, 3)), DMA((4,)), DMA((4,)), DMA((4, 3)), DMA((4, 3)),
             DMA((12,)),
-            pltpu.VMEM((4, ROWS, 192), bf16),
-            pltpu.VMEM((4, ROWS, 192), bf16),
-            DMA((3,)), DMA((3,)),
+            pltpu.VMEM((4, ROWS, 128), bf16),
+            pltpu.VMEM((4, ROWS, 128), bf16),
+            pltpu.VMEM((4, 200, 128), bf16),
+            pltpu.VMEM((4, 200, 128), bf16),
+            DMA((2, 3)), DMA((2, 3)),
         ],
         name="attention_backward",
         compiler_params=pltpu.CompilerParams(

time: 173 us -> 173 us (level)
  no operation moved by 1% of the time
where the time goes in v5:
time: 173 us
  Pallas kernels  170 us (98%)
    pallas_call x1, Pallas kernels, backward_call(): pl.pallas_call(backward_kernel, out_shape=(shape((ROWS, D), f32), shape((...  80.1 us
    pallas_call x1, Pallas kernels, forward_call(): pl.pallas_call(forward_kernel, out_shape=(shape((8, D + UNITS), f32),) +...  62.8 us
    pallas_call x1, Pallas kernels, feed_forward_call(): pl.pallas_call(feed_forward_kernel, out_shape=(shape((ROWS, D), f32), sha...  23 us
    pallas_call x1, Pallas kernels, results_call(): pl.pallas_call(results_kernel, out_shape=(shape((ROWS, D), f32), shape((R...  4.56 us

profile of v5, /device:TPU:0, one launch (start us, length us, event | category | flops | bytes accessed | tf_op | source)
XLA Modules:
  0.0 172.7 jit_solution(4321258156615869933)
XLA Ops:
  0.6 1.4 stack.32.small
  2.0 62.8 %attention_forward.1 = (f32[8,1152]{1,0:T(8,128)}, bf16[2,784,768]{2,1,0:T(8,128)(2,1)}, bf16[9,1568,64]{2,1,0:T(8,128)(2,1)}, f32[21,8,224]{2,1,0:T(8,128)}, f3...) custom-call(bf16[8,6]{1,0:T(8,128)(2,1)} %stack.32.small, ...), custom_call_target="tpu_custom_call" | custom-call | tf_op jit(solution)/shard_map/attention_forward/pallas_call | solution.py:495
  64.8 23.0 %feed_forward.1 = (f32[392,768]{1,0:T(8,128)}, f32[392,768]{1,0:T(8,128)}, bf16[392,768]{1,0:T(8,128)(2,1)}, bf16[4,392,128]{2,1,0:T(8,128)(2,1)}, bf16[4,392,64...) custom-call(s32[1,196]{1,0:T(1,128)} %cubes.5, f32[8,1152]{1,0:T(8,128)} %get-tuple-element.55.params, ...), custom_call_target="tpu_custom_call" | custom-call | tf_op jit(solution)/shard_map/feed_forward/pallas_call | solution.py:651
  87.8 80.1 %attention_backward.1 = (f32[392,768]{1,0:T(8,128)}, f32[8,1152]{1,0:T(8,128)}, f32[8,640]{1,0:T(8,128)}, bf16[4,4,288,128]{3,2,1,0:T(8,128)(2,1)}, f32[24,768]{1,0:T(8,128)}, /*index=5*/f32[24,768]{1,0:T(8,128)}) custom-call(s32[1,196]{1,0:T(1,128)} %cubes.5, f32[8,1152]{1,0:T(8,128)} %get-tuple-element.55.params, ...), custom_call_target="tpu_custom_call" | custom-call | tf_op jit(solution)/shard_map/attention_backward/pallas_call | solution.py:1145
  168.0 4.6 %results.1 = (f32[392,768]{1,0:T(8,128)}, f32[392,768]{1,0:T(8,128)}, f32[1,6]{1,0:T(1,128)}, f32[1,6]{1,0:T(1,128)}, f32[1,6]{1,0:T(1,128)}, /*index=5*/f32[576...) custom-call(f32[392,768]{1,0:T(8,128)} %get-tuple-element.60.block_i, ...), custom_call_target="tpu_custom_call" | custom-call | tf_op jit(solution)/shard_map/results/pallas_call | solution.py:1258

commit v6 on v5

--- a/solution.py
+++ b/solution.py
@@ -988,20 +988,20 @@
 
         column_sums[pl.ds(h, 1), :] = jnp.sum(packed_back[...].astype(f32), axis=0, keepdims=True)
 
+        w_grad = dot_tn(packed_back[...], normed[...])
+        for n in range(HEADS_HERE):
+            pl.when(h == n)(partial(w_begin, n + 1, w_grad))
+
+        @pl.when(h == 0)
+        def _():
+            outer_in(1)
+            sum_on(0)
+
         @pl.when(h == HEADS_HERE - 2)
         def _():
             pair_copies[0].wait_recv()
             far_out[...] = (input_back[1 - chip, core] + pair_in[0].astype(f32)).astype(bf16)
             far_copy.start()
-
-        w_grad = dot_tn(packed_back[...], normed[...])
-        for n in range(HEADS_HERE):
-            pl.when(h == n)(partial(w_begin, n + 1, w_grad))
-
-        @pl.when(h == 0)
-        def _():
-            outer_in(1)
-            sum_on(0)
 
         @pl.when(h == 1)
         def _():
@@ -1029,10 +1029,10 @@
 
     lax.fori_loop(0, HEADS_HERE, attend, 0)
 
+    ff_on(0)
     branch_end()
     w_second(1)
     w_second(2)
-    ff_on(0)
     sum_on(2)
     w_second(3)
     w_third(1)

time: 173 us -> 172 us (level)
  no operation moved by 1% of the time
where the time goes in v6:
time: 172 us; the launch traced here: 171 us
  Pallas kernels  169 us (98%)
    pallas_call x1, Pallas kernels, backward_call(): pl.pallas_call(backward_kernel, out_shape=(shape((ROWS, D), f32), shape((...  78.7 us
    pallas_call x1, Pallas kernels, forward_call(): pl.pallas_call(forward_kernel, out_shape=(shape((8, D + UNITS), f32),) +...  62.8 us
    pallas_call x1, Pallas kernels, feed_forward_call(): pl.pallas_call(feed_forward_kernel, out_shape=(shape((ROWS, D), f32), sha...  23 us
    pallas_call x1, Pallas kernels, results_call(): pl.pallas_call(results_kernel, out_shape=(shape((ROWS, D), f32), shape((R...  4.56 us

profile of v6, /device:TPU:0, one launch (start us, length us, event | category | flops | bytes accessed | tf_op | source)
XLA Modules:
  0.0 171.3 jit_solution(11578027835596908768)
XLA Ops:
  0.6 1.4 stack.32.small
  2.0 62.8 %attention_forward.1 = (f32[8,1152]{1,0:T(8,128)}, bf16[2,784,768]{2,1,0:T(8,128)(2,1)}, bf16[9,1568,64]{2,1,0:T(8,128)(2,1)}, f32[21,8,224]{2,1,0:T(8,128)}, f3...) custom-call(bf16[8,6]{1,0:T(8,128)(2,1)} %stack.32.small, ...), custom_call_target="tpu_custom_call" | custom-call | tf_op jit(solution)/shard_map/attention_forward/pallas_call | solution.py:495
  64.8 23.0 %feed_forward.1 = (f32[392,768]{1,0:T(8,128)}, f32[392,768]{1,0:T(8,128)}, bf16[392,768]{1,0:T(8,128)(2,1)}, bf16[4,392,128]{2,1,0:T(8,128)(2,1)}, bf16[4,392,64...) custom-call(s32[1,196]{1,0:T(1,128)} %cubes.5, f32[8,1152]{1,0:T(8,128)} %get-tuple-element.55.params, ...), custom_call_target="tpu_custom_call" | custom-call | tf_op jit(solution)/shard_map/feed_forward/pallas_call | solution.py:651
  87.8 78.7 %attention_backward.1 = (f32[392,768]{1,0:T(8,128)}, f32[8,1152]{1,0:T(8,128)}, f32[8,640]{1,0:T(8,128)}, bf16[4,4,288,128]{3,2,1,0:T(8,128)(2,1)}, f32[24,768]{1,0:T(8,128)}, /*index=5*/f32[24,768]{1,0:T(8,128)}) custom-call(s32[1,196]{1,0:T(1,128)} %cubes.5, f32[8,1152]{1,0:T(8,128)} %get-tuple-element.55.params, ...), custom_call_target="tpu_custom_call" | custom-call | tf_op jit(solution)/shard_map/attention_backward/pallas_call | solution.py:1145
  166.5 4.6 %results.1 = (f32[392,768]{1,0:T(8,128)}, f32[392,768]{1,0:T(8,128)}, f32[1,6]{1,0:T(1,128)}, f32[1,6]{1,0:T(1,128)}, f32[1,6]{1,0:T(1,128)}, /*index=5*/f32[576...) custom-call(f32[392,768]{1,0:T(8,128)} %get-tuple-element.60.block_i, ...), custom_call_target="tpu_custom_call" | custom-call | tf_op jit(solution)/shard_map/results/pallas_call | solution.py:1258
